TPU v7x, 512 devices: a whole 4x4x16 slice. The times are simulated.
512 devices in a mesh: sec: 4 (over z_hi), seq: 128 (over z_lo, x, y, core).
Axes of the slice: x: 4, y: 4, z: 16 (z_hi: 4, z_lo: 4; z = z_hi * 4 + z_lo), core: 2. Of those that a mesh axis runs over, the one named last changes fastest.
Arguments:
- video: bfloat16 [3, 128, 512, 256], P(None, 'seq', 'sec'), may hold values from -6 to 6
- conv_weight: bfloat16 [128, 81], replicated, may hold values from -0.625 to 0.625
- down_weight: bfloat16 [128, 8, 8, 16], replicated, may hold values from -0.0625 to 0.0625
- noise: bfloat16 [16, 128, 64, 32], P(None, 'seq', 'sec'), may hold values from -6 to 6
- timesteps: int32 [128], P('seq'), may hold values from 0 to 999
- embed_weight: bfloat16 [64, 3072], replicated, may hold values from -0.75 to 0.75
- mod_weight: bfloat16 [256, 3072], replicated, may hold values from -0.375 to 0.375
- qkv_weight: bfloat16 [3072, 12, 384], P('seq', 'sec'), may hold values from -0.109375 to 0.109375
- cotangent: bfloat16 [128, 512, 1536], P('seq', 'sec'), may hold values from -24 to 24
Outputs:
- latents: bfloat16 [16, 128, 64, 32], P(None, 'seq', 'sec')
- attended: bfloat16 [128, 512, 1536], P('seq', 'sec')
- out_grad: float32 [1536, 1536], P('seq', 'sec')
All inputs are finite; a program needn't handle non-finite values.
Results may differ from a plain program's by a relative error of at most 0.01.
Values may be sent and summed in bfloat16 or wider, within the bound.
No kernel may reach another device: no remote copies, remote signals or barrier semaphores. Data moves between devices by JAX's collectives and lax.ppermute only.
A program may use at most 128 MiB of HBM per device.

v0:
```python
import math

import jax
import jax.numpy as jnp
from jax import lax
from jax.sharding import PartitionSpec as P

STEPS = 1000


def from_behind(shard, axis, by):
    size = lax.axis_size(axis)
    pairs = [(i, i + by) for i in range(size) if 0 <= i + by < size]
    return lax.ppermute(shard, axis, pairs)


def padded_2(shard, sides, width):
    for axis, dim in sides:
        size, length = (lax.axis_size(axis), shard.shape[dim])
        up = [(i, (i + 1) % size) for i in range(size - 1)]
        down = [(j, i) for i, j in up]
        last = lax.slice_in_dim(shard, length - width, length, axis=dim)
        initial = lax.slice_in_dim(shard, 0, width, axis=dim)
        before = lax.ppermute(last, axis, up)
        after = lax.ppermute(initial, axis, down)
        shard = jnp.concatenate([before, shard, after], axis=dim)
    return shard


def encode_rows(pixels, conv_weight, down_weight):
    channels = pixels.shape[0]
    height = pixels.shape[2] - 2
    breadth = pixels.shape[3] - 2
    windows = []
    for channel in range(channels):
        for shift_t in range(3):
            for shift_y in range(3):
                for shift_x in range(3):
                    windows.append(
                        pixels[
                            channel,
                            shift_t,
                            shift_y : shift_y + height,
                            shift_x : shift_x + breadth,
                        ]
                    )
    columns = jnp.stack(windows).reshape(len(windows), height * breadth)
    before = jnp.dot(conv_weight, columns, preferred_element_type=jnp.float32)
    feature = jax.nn.silu(before).astype(jnp.bfloat16)
    feature = feature.reshape(feature.shape[0], height // 8, 8, breadth // 8, 8)
    latent = jnp.einsum("caiej,cijl->lae", feature, down_weight, preferred_element_type=jnp.float32)
    return latent.astype(jnp.bfloat16)


def noisy_latents(latents, noise, timesteps):
    noise_level = (timesteps.astype(jnp.float32) + 1.0) / STEPS
    noise_level = noise_level[None, :, None, None]
    blended = (1.0 - noise_level) * latents.astype(jnp.float32) + noise_level * noise.astype(
        jnp.float32
    )
    return blended.astype(jnp.bfloat16)


def frame_patches(noised):
    channels, lat_rows, lat_cols = noised.shape
    blocks = noised.reshape(channels, lat_rows // 2, 2, lat_cols // 2, 2).transpose(1, 3, 0, 2, 4)
    return blocks.reshape(lat_rows // 2 * (lat_cols // 2), channels * 4)


def modulation(timesteps, mod_weight):
    half_width = mod_weight.shape[0] // 2
    frequency = jnp.exp(-math.log(10000.0) * jnp.arange(half_width, dtype=jnp.float32) / half_width)
    angles = timesteps.astype(jnp.float32)[:, None] * frequency[None, :]
    embedded = jnp.concatenate([jnp.cos(angles), jnp.sin(angles)], axis=1)
    return jnp.dot(embedded, mod_weight.astype(jnp.float32), precision=lax.Precision.HIGHEST)


def prepare(patches, embed_weight, mod_scale):
    embedded = jnp.dot(patches, embed_weight, preferred_element_type=jnp.float32)
    center = embedded - jnp.mean(embedded, axis=1, keepdims=True)
    spread = jnp.mean(center * center, axis=1, keepdims=True)
    normed = center * lax.rsqrt(spread + 1e-06) * (1.0 + mod_scale)
    return normed.astype(jnp.bfloat16)


def attention(projected):
    head_size = projected.shape[3]
    queries = projected[:, :, 0]
    key_rows = projected[:, :, 1]
    values = projected[:, :, 2]
    scores = jnp.einsum(
        "qhd,khd->hqk", queries, key_rows, preferred_element_type=jnp.float32
    ) / math.sqrt(head_size)
    attn_probs = jax.nn.softmax(scores, axis=-1).astype(jnp.bfloat16)
    output = jnp.einsum("hqk,khd->qhd", attn_probs, values, preferred_element_type=jnp.float32)
    return output.astype(jnp.bfloat16).reshape(projected.shape[0], projected.shape[1] * head_size)


def on_device(
    video,
    conv_weight,
    down_weight,
    noise,
    timesteps,
    embed_weight,
    mod_weight,
    qkv_weight,
    cotangent,
):
    earlier = [from_behind(video, "seq", offset) for offset in (2, 1)]
    stacked = jnp.concatenate(earlier + [video], axis=1)
    rimmed = padded_2(stacked, (("sec", 2),), 1)
    padded = jnp.pad(rimmed, ((0, 0), (0, 0), (0, 0), (1, 1)))
    band_rows = video.shape[2]
    row_block = math.gcd(band_rows, 64)
    pieces = []
    for first_row in range(0, band_rows, row_block):
        pixels = padded[:, :, first_row : first_row + row_block + 2]
        pieces.append(encode_rows(pixels, conv_weight, down_weight))
    latents = jnp.concatenate(pieces, axis=1)[:, None]
    noised = noisy_latents(latents, noise, timesteps)
    patches = frame_patches(noised[:, 0])
    mod_scale = modulation(timesteps, mod_weight)
    grouped = lax.all_gather(prepare(patches, embed_weight, mod_scale), "sec", axis=0, tiled=True)
    heads_here = qkv_weight.shape[1]
    row_span = heads_here * qkv_weight.shape[2]
    weight_rows = lax.all_gather(qkv_weight, "seq", axis=0, tiled=True)
    qkv_total = jnp.dot(
        grouped,
        weight_rows.reshape(weight_rows.shape[0], row_span),
        preferred_element_type=jnp.float32,
    )
    head_size = qkv_weight.shape[2] // 3
    projected = qkv_total.astype(jnp.bfloat16).reshape(grouped.shape[0], heads_here, 3, head_size)
    heads_out = attention(projected)
    attended = lax.all_to_all(heads_out, "sec", split_axis=0, concat_axis=1, tiled=True)
    grads_in = lax.all_gather(cotangent[0], "sec", axis=0, tiled=True)
    out_grad = lax.psum_scatter(
        lax.dot_general(
            grads_in, heads_out, (((0,), (0,)), ((), ())), preferred_element_type=jnp.float32
        ),
        "seq",
        scatter_dimension=0,
        tiled=True,
    )
    return (latents, attended[None], out_grad)


def solution(mesh):
    in_specs = (
        P(None, "seq", "sec", None),
        P(),
        P(),
        P(None, "seq", "sec", None),
        P("seq"),
        P(),
        P(),
        P("seq", "sec", None),
        P("seq", "sec", None),
    )
    out_specs = (P(None, "seq", "sec", None), P("seq", "sec", None), P("seq", "sec"))
    return jax.shard_map(
        on_device, mesh=mesh, in_specs=in_specs, out_specs=out_specs, check_vma=False
    )
```

profile of v0, /device:TPU:1, one launch (start us, length us, event | category | flops | bytes accessed | tf_op | source)
XLA Modules:
  0.0 1719.0 jit_solution(6326683972602496759)
XLA Ops:
  8.0 4.0 collective-permute-start
  12.0 4.0 collective-permute-start.1
  19.3 1.5 collective-permute-done.1
  20.9 7.3 collective-permute-start.2
  28.2 1.3 collective-permute-start.3
  34.7 3.4 collective-permute-done.3
  124.7 24.1 %stack.411 = bf16[81,16384]{1,0:T(8,128)(2,1)} concatenate(bf16[1,16384]{1,0:T(2,128)(2,1)} %bitcast.825, bf16[1,16384]{1,0:T(2,128)(2,1)} %bitcast.859, bf16[1,16384]{1,0:T(2,128)(2,1)} %bitcast.826, bf16[1,16384]{1,0:T(2,128)(2,1)} %bitcast.827, bf16[1,16384]{1,0:T(2,128)(2,1)S(1)} %bitcast.778, bf16[1,16384]{1,0:T(2,128)(2,1)} %bitcast.828, bf16[1,16384]{1,0:T(2,128)(2,1)} %bitcast.829, ...), dimensions={0} | concatenate | bytes 5308416 | tf_op jit(solution)/shard_map/stack | solution.py:47
  148.9 24.1 %stack.493 = bf16[81,16384]{1,0:T(8,128)(2,1)} concatenate(bf16[1,16384]{1,0:T(2,128)(2,1)S(1)} %bitcast.836, bf16[1,16384]{1,0:T(2,128)(2,1)S(1)} %bitcast.758, bf16[1,16384]{1,0:T(2,128)(2,1)S(1)} %bitcast.837, bf16[1,16384]{1,0:T(2,128)(2,1)S(1)} %bitcast.838, bf16[1,16384]{1,0:T(2,128)(2,1)S(1)} %bitcast.759, bf16[1,16384]{1,0:T(2,128)(2,1)S(1)} %bitcast.839, ...), dimensions={0} | concatenate | bytes 5308416 | tf_op jit(solution)/shard_map/stack | solution.py:47
  173.1 4.5 multiply_convert_fusion.1
  177.6 2.8 fusion.22
  180.4 2.6 multiply_convert_fusion
  183.0 2.8 fusion.19
  189.2 35.3 %all-gather.7.cloned.1.call-done = bf16[3072,3,384]{2,0,1:T(8,128)(2,1)} async-done(((bf16[24,3,384]{2,0,1:T(8,128)(2,1)}), bf16[3072,3,384]{2,0,1:T(8,128)(2,1)}) %all-gather.7.cloned.1.call-update) | async-done | bytes 7077904 | tf_op jit(solution)/shard_map/all_gather | solution.py:127
  224.5 10.5 copy.41
  235.0 118.8 %all-gather.5.cloned.1.call-done = bf16[512,3072]{1,0:T(8,128)(2,1)} async-done(((bf16[128,3072]{1,0:T(8,128)(2,1)}), bf16[512,3072]{1,0:T(8,128)(2,1)}) %all-gather.5.cloned.1.call-update) | async-done | bytes 3145744 | tf_op jit(solution)/shard_map/all_gather | solution.py:124
  353.7 8.2 convolution_convert_fusion
  363.2 1.6 copy-done.2
  365.7 4.1 fusion.12
  369.9 58.1 %all-gather.9.cloned.1.call-done = bf16[1,512,1536]{2,1,0:T(8,128)(2,1)} async-done(((bf16[1,128,1536]{2,1,0:T(8,128)(2,1)}), bf16[1,512,1536]{2,1,0:T(8,128)(2,1)}) %all-gather.9.cloned.1.call-update) | async-done | bytes 1572880 | tf_op jit(solution)/shard_map/all_gather | solution.py:137
  428.0 3.6 convolution_bitcast_fusion.2
  432.5 7.3 all-to-all-start
  439.8 1.3 dynamic-slice
  442.4 19.1 %all-to-all-done = bf16[4,128,384]{1,2,0:T(8,128)(2,1)S(1)} async-done(((bf16[4,128,384]{1,2,0:T(8,128)(2,1)}), bf16[4,128,384]{1,2,0:T(8,128)(2,1)S(1)}, u32[]{:S(2)}, u32[]{:S(2)}) %all-to-all-start) | async-done | bytes 393248 | tf_op jit(solution)/shard_map/all_to_all | solution.py:136
  462.4 1247.7 %all-reduce.4.cloned.1.call-done = f32[1536,384]{0,1:T(8,128)} async-done(((f32[1536,384]{0,1:T(8,128)}), f32[1536,384]{0,1:T(8,128)}) %all-reduce.4.cloned.1.call-update) | async-done | bytes 2359312
  (275 shorter events, 104.4 us)
Async XLA Ops:
  7.2 217.3 %all-gather.7.cloned.1.call-start = ((), (), s32[]{:S(2)}) async-start(), calls=%async_computation.2 | async-start | bytes 7133184 | tf_op jit(solution)/shard_map/all_gather | solution.py:127
  7.9 345.8 %all-gather.5.cloned.1.call-start = ((), (), s32[]{:S(2)}) async-start(), calls=%async_computation.1 | async-start | bytes 3932160 | tf_op jit(solution)/shard_map/all_gather | solution.py:124
  8.0 11.3 collective-permute-start
  12.0 8.8 collective-permute-start.1
  20.9 13.8 collective-permute-start.2
  28.2 9.9 collective-permute-start.3
  89.5 35.0 %copy-start.7 = (bf16[1,1,64,256]{3,1,2,0:T(2,128)(2,1)S(1)}, bf16[1,1,64,256]{3,1,2,0:T(2,128)(2,1)}, u32[]{:S(2)}) copy-start(bf16[1,1,64,256]{3,1,2,0:T(2,128)(2,1)} %copy.129) | copy-start | bytes 98308
  89.5 35.0 %copy-start.8 = (bf16[1,1,64,256]{3,1,2,0:T(2,128)(2,1)S(1)}, bf16[1,1,64,256]{3,1,2,0:T(2,128)(2,1)}, u32[]{:S(2)}) copy-start(bf16[1,1,64,256]{3,1,2,0:T(2,128)(2,1)} %copy.63) | copy-start | bytes 98308
  89.5 35.0 %copy-start.9 = (bf16[1,1,64,256]{3,1,2,0:T(2,128)(2,1)S(1)}, bf16[1,1,64,256]{3,1,2,0:T(2,128)(2,1)}, u32[]{:S(2)}) copy-start(bf16[1,1,64,256]{3,1,2,0:T(2,128)(2,1)} %copy.66) | copy-start | bytes 98308
  89.5 35.0 %copy-start.10 = (bf16[1,1,64,256]{3,1,2,0:T(2,128)(2,1)S(1)}, bf16[1,1,64,256]{3,1,2,0:T(2,128)(2,1)}, u32[]{:S(2)}) copy-start(bf16[1,1,64,256]{3,1,2,0:T(2,128)(2,1)} %copy.72) | copy-start | bytes 98308
  89.5 35.0 %copy-start.11 = (bf16[1,1,64,256]{3,1,2,0:T(2,128)(2,1)S(1)}, bf16[1,1,64,256]{3,1,2,0:T(2,128)(2,1)}, u32[]{:S(2)}) copy-start(bf16[1,1,64,256]{3,1,2,0:T(2,128)(2,1)} %copy.75) | copy-start | bytes 98308
  89.6 35.0 %copy-start.12 = (bf16[1,1,64,256]{3,1,2,0:T(2,128)(2,1)S(1)}, bf16[1,1,64,256]{3,1,2,0:T(2,128)(2,1)}, u32[]{:S(2)}) copy-start(bf16[1,1,64,256]{3,1,2,0:T(2,128)(2,1)} %copy.77) | copy-start | bytes 98308
  89.6 35.0 %copy-start.13 = (bf16[1,1,64,256]{3,1,2,0:T(2,128)(2,1)S(1)}, bf16[1,1,64,256]{3,1,2,0:T(2,128)(2,1)}, u32[]{:S(2)}) copy-start(bf16[1,1,64,256]{3,1,2,0:T(2,128)(2,1)} %copy.79) | copy-start | bytes 98308
  89.6 35.0 %copy-start.14 = (bf16[1,1,64,256]{3,1,2,0:T(2,128)(2,1)S(1)}, bf16[1,1,64,256]{3,1,2,0:T(2,128)(2,1)}, u32[]{:S(2)}) copy-start(bf16[1,1,64,256]{3,1,2,0:T(2,128)(2,1)} %copy.80) | copy-start | bytes 98308
  89.6 35.0 %copy-start.15 = (bf16[1,1,64,256]{3,1,2,0:T(2,128)(2,1)S(1)}, bf16[1,1,64,256]{3,1,2,0:T(2,128)(2,1)}, u32[]{:S(2)}) copy-start(bf16[1,1,64,256]{3,1,2,0:T(2,128)(2,1)} %copy.82) | copy-start | bytes 98308
  89.6 35.0 %copy-start.16 = (bf16[1,1,64,256]{3,1,2,0:T(2,128)(2,1)S(1)}, bf16[1,1,64,256]{3,1,2,0:T(2,128)(2,1)}, u32[]{:S(2)}) copy-start(bf16[1,1,64,256]{3,1,2,0:T(2,128)(2,1)} %copy.83) | copy-start | bytes 98308
  89.6 35.0 %copy-start.17 = (bf16[1,1,64,256]{3,1,2,0:T(2,128)(2,1)S(1)}, bf16[1,1,64,256]{3,1,2,0:T(2,128)(2,1)}, u32[]{:S(2)}) copy-start(bf16[1,1,64,256]{3,1,2,0:T(2,128)(2,1)} %copy.85) | copy-start | bytes 98308
  89.6 35.0 %copy-start.18 = (bf16[1,1,64,256]{3,1,2,0:T(2,128)(2,1)S(1)}, bf16[1,1,64,256]{3,1,2,0:T(2,128)(2,1)}, u32[]{:S(2)}) copy-start(bf16[1,1,64,256]{3,1,2,0:T(2,128)(2,1)} %copy.86) | copy-start | bytes 98308
  89.6 35.0 %copy-start.19 = (bf16[1,1,64,256]{3,1,2,0:T(2,128)(2,1)S(1)}, bf16[1,1,64,256]{3,1,2,0:T(2,128)(2,1)}, u32[]{:S(2)}) copy-start(bf16[1,1,64,256]{3,1,2,0:T(2,128)(2,1)} %copy.88) | copy-start | bytes 98308
  89.6 35.0 %copy-start.20 = (bf16[1,1,64,256]{3,1,2,0:T(2,128)(2,1)S(1)}, bf16[1,1,64,256]{3,1,2,0:T(2,128)(2,1)}, u32[]{:S(2)}) copy-start(bf16[1,1,64,256]{3,1,2,0:T(2,128)(2,1)} %copy.89) | copy-start | bytes 98308
  188.4 239.5 %all-gather.9.cloned.1.call-start = ((), (), s32[]{:S(2)}) async-start(), calls=%async_computation.3 | async-start | bytes 1966080 | tf_op jit(solution)/shard_map/all_gather | solution.py:137
  189.2 1521.0 %all-reduce.4.cloned.1.call-start = ((), (), s32[]{:S(2)}) async-start(), calls=%async_computation.4 | async-start | bytes 4718592
  431.6 1280.4 %copy-start.1 = (bf16[256,3072]{1,0:T(8,128)(2,1)S(1)}, bf16[256,3072]{1,0:T(8,128)(2,1)}, u32[]{:S(2)}) copy-start(bf16[256,3072]{1,0:T(8,128)(2,1)} %param.15) | copy-start | bytes 4718596
  432.5 29.0 %all-to-all-start = ((bf16[4,128,384]{1,2,0:T(8,128)(2,1)}), bf16[4,128,384]{1,2,0:T(8,128)(2,1)S(1)}, u32[]{:S(2)}, u32[]{:S(2)}) async-start(bf16[4,128,384]{1,2,0:T(8,128)(2,1)} %copy.47), calls=%async_computation | async-start | bytes 786432 | tf_op jit(solution)/shard_map/all_to_all | solution.py:136
  (18 other events, 316.6 us)
Sparse Core Ops, SparseCore 0:
  10.1 214.3 all-gather.6
  226.6 127.0 all-gather.4
  355.9 72.0 all-gather.8
  431.7 1278.3 all-reduce.3
where the time goes:
time: 1730 us; the launch traced here: 1720 us
  waiting for transfers between devices  1490 us (86%)
  local copies, waits for them, and re-layouts  159 us (9%)
  matrix products  30.4 us (2%)
  starting transfers between devices  24.2 us (1%)
    unnamed x5, waiting for transfers between devices  1250 us
    all_gather x1, waiting for transfers between devices, on_device(): lax.all_gather(prepare(patches, embed_weight, mod_scale), 'sec', axis=0,...  119 us
    unnamed x244, local copies, waits for them, and re-layouts  98.5 us
    all_gather x1, waiting for transfers between devices, on_device(): grads_in = lax.all_gather(cotangent[0], 'sec', axis=0, tiled=True)  58.1 us
    another operation x2, local copies, waits for them, and re-layouts, encode_rows(): columns = jnp.stack(windows).reshape(len(windows), height * breadth)  48.3 us
    all_gather x1, waiting for transfers between devices, on_device(): weight_rows = lax.all_gather(qkv_weight, 'seq', axis=0, tiled=True)  35.3 us
  transfers between devices with their start and end apart: 9, of which 7 were waited for; matrix products, arithmetic and copies ran while one was open for 11% of the time, Pallas kernels for 0%

commit v1 on v0

v1 whole, which is shorter than its diff:
```python
import math

import jax
import jax.numpy as jnp
from jax import lax
from jax.experimental import pallas as pl
from jax.experimental.pallas import tpu as pltpu
from jax.sharding import Mesh, PartitionSpec as P

STEPS = 1000
SEQ = ("zl", "x", "y", "core")
F32 = jnp.float32
BF16 = jnp.bfloat16
VMEM = pl.BlockSpec(memory_space=pltpu.VMEM)
SMEM = pl.BlockSpec(memory_space=pltpu.SMEM)
VMEM_BYTES = 48 * 1024 * 1024


def call(body, out_shape, n_smem, n_vmem, flops, nbytes, scratch=()):
    several = isinstance(out_shape, (list, tuple))
    return pl.pallas_call(
        body,
        out_shape=out_shape,
        in_specs=[SMEM] * n_smem + [VMEM] * n_vmem,
        out_specs=[VMEM] * len(out_shape) if several else VMEM,
        scratch_shapes=list(scratch),
        compiler_params=pltpu.CompilerParams(vmem_limit_bytes=VMEM_BYTES),
        cost_estimate=pl.CostEstimate(flops=flops, bytes_accessed=nbytes, transcendentals=0),
    )


def iota(shape, dim):
    return lax.broadcasted_iota(jnp.int32, shape, dim)


def one_hot(where):
    return jnp.where(where, 1.0, 0.0).astype(BF16)


def prep_body(place, embed, mod, temb, a_hi, a_lo, gram):
    core = place[0]
    start = pl.multiple_of(place[1] * 768, 128)
    to, of = iota((64, 64), 0), iota((64, 64), 1)
    order = one_hot(of == (to & 15) * 4 + ((to >> 4) & 1) * 2 + (to >> 5))
    emb = jnp.dot(order, embed[...], preferred_element_type=F32)
    mean = jnp.mean(emb, axis=1, keepdims=True)
    center = emb - mean
    gram[...] = (
        lax.dot_general(
            center,
            center,
            (((1,), (1,)), ((), ())),
            precision=lax.Precision.HIGHEST,
            preferred_element_type=F32,
        )
        / embed.shape[1]
    )
    col = iota((768, 384), 1)
    block = (col * 2731) >> 16
    pick = one_hot(iota((768, 384), 0) == 24 * block + 24 * core + col)
    emb_part = jnp.dot(order, embed[:, pl.ds(start, 768)], preferred_element_type=F32)
    emb_pick = jnp.dot(emb_part.astype(BF16), pick, preferred_element_type=F32) - mean
    mod_pick = jnp.dot(mod[:, pl.ds(start, 768)], pick, preferred_element_type=F32).astype(BF16)
    t = temb[...]
    first = t.astype(BF16).astype(F32)
    second = (t - first).astype(BF16).astype(F32)
    third = t - first - second
    pieces = jnp.concatenate([first, second, third], axis=0).astype(BF16)
    scale = jnp.dot(pieces, mod_pick, preferred_element_type=F32)
    scale = 1.0 + (scale[0:8] + scale[8:16] + scale[16:24])
    for f in range(8):
        a = emb_pick * scale[f : f + 1]
        hi = a.astype(BF16)
        a_hi[64 * f : 64 * f + 64] = hi
        a_lo[64 * f : 64 * f + 64] = (a - hi.astype(F32)).astype(BF16)


def fold_body(a_hi, a_lo, w, keep, send):
    for h in range(3):
        for out, rows in ((send, slice(256, 512)), (keep, slice(0, 256))):
            out[:, 384 * h : 384 * h + 384] = jnp.dot(
                a_hi[rows], w[h], preferred_element_type=F32
            ) + jnp.dot(a_lo[rows], w[h], preferred_element_type=F32)


def encode_body(level, v2, v1, v0, conv, down, noise, lat, pat, s32, s16, rows_out):
    x = iota((136, 256), 1)
    for c in range(3):
        for dt, v in enumerate((v2, v1, v0)):
            img = v[c, 0].astype(F32)
            left = jnp.where(x[:130] == 0, 0.0, pltpu.roll(img, 1, 1))
            right = jnp.where(x[:130] == 255, 0.0, pltpu.roll(img, 255, 1))
            for dx, shifted in enumerate((left, img, right)):
                k = dx * 9 + c * 3 + dt
                for half in range(2):
                    part = shifted[:, 128 * half : 128 * half + 128]
                    s32[half, pl.ds(32 + k, 128, stride=32), :] = part[0:128]
                    s32[half, pl.ds(129 * 32 + k, 1), :] = part[128:129]
                    s32[half, pl.ds(k, 1), :] = part[129:130]
    for k in range(27, 32):
        for half in range(2):
            s32[half, pl.ds(k, 130, stride=32), :] = jnp.zeros((130, 128), F32)

    def pack(i, _):
        rows = pl.ds(pl.multiple_of(i * 320, 64), 320)
        for half in range(2):
            s16[rows, 128 * half : 128 * half + 128] = s32[half, rows, :].astype(BF16)
        return 0

    lax.fori_loop(0, 13, pack, 0)
    own_lane = (iota((128, 256), 1) & 7) == (iota((128, 256), 0) >> 4)

    def block_row(a, _):
        feats = []
        for q in range(4):
            taps = s16[pl.ds(pl.multiple_of(a * 256 + 64 * q, 64), 128), :]
            pre = jnp.dot(conv[...], taps, preferred_element_type=F32)
            half = 0.5 * pre
            feats.append((half + half * jnp.tanh(half)).astype(BF16))
        feature = jnp.concatenate(feats, axis=0)
        weights = jnp.concatenate([down[i] for i in range(8)], axis=1)
        prod = jnp.dot(weights, feature, preferred_element_type=F32)
        prod = jnp.where(own_lane, prod, 0.0)
        acc = prod[0:16]
        for j in range(1, 8):
            acc = acc + prod[16 * j : 16 * j + 16]
        for by in (1, 2, 4):
            acc = acc + pltpu.roll(acc, 256 - by, 1)
        rows_out[pl.ds(pl.multiple_of(a * 16, 16), 16), :] = acc.astype(BF16)
        return 0

    lax.fori_loop(0, 16, block_row, 0)
    pick = one_hot(iota((256, 32), 0) == 8 * iota((256, 32), 1))
    lat[...] = jnp.dot(rows_out[...], pick, preferred_element_type=F32).astype(BF16)
    px, tok = iota((256, 128), 0), iota((256, 128), 1)
    for w in range(2):
        acc = jnp.zeros((32, 128), F32)
        for r in range(8):
            place = one_hot((px == 16 * (tok & 15) + 8 * w) & ((tok >> 4) == r))
            acc = acc + jnp.dot(
                rows_out[32 * r : 32 * r + 32], place, preferred_element_type=F32
            )
        t = level[0]
        mixed = (1.0 - t) * acc + t * noise[32 * w : 32 * w + 32].astype(F32)
        pat[32 * w : 32 * w + 32] = mixed.astype(BF16)


def attend_body(pats, parts, gram, att):
    tokens_t = jnp.concatenate([pats[s] for s in range(4)], axis=1).astype(F32)
    tokens = tokens_t.T
    spread = jnp.sum(
        tokens
        * jnp.dot(
            tokens, gram[...], precision=lax.Precision.HIGHEST, preferred_element_type=F32
        ),
        axis=1,
        keepdims=True,
    )
    scale = lax.rsqrt(spread + 1e-06)
    total = (parts[0].astype(F32) + parts[1].astype(F32)) + (
        parts[2].astype(F32) + parts[3].astype(F32)
    )
    hi = total.astype(BF16)
    lo = (total - hi.astype(F32)).astype(BF16)
    weights = jnp.concatenate([hi, lo], axis=0)
    twice = jnp.concatenate([tokens, tokens], axis=1).astype(BF16)
    for h in range(3):
        proj = jnp.dot(
            twice, weights[:, 384 * h : 384 * h + 384], preferred_element_type=F32
        )
        proj = (proj * scale).astype(BF16)
        q, k, v = proj[:, 0:128], proj[:, 128:256], proj[:, 256:384]
        scores = lax.dot_general(
            q, k, (((1,), (1,)), ((), ())), preferred_element_type=F32
        ) * (1.0 / math.sqrt(128.0))
        probs = jnp.exp(scores - jnp.max(scores, axis=1, keepdims=True))
        norm = 1.0 / jnp.sum(probs, axis=1, keepdims=True)
        out = jnp.dot(probs.astype(BF16), v, preferred_element_type=F32) * norm
        att[:, 128 * h : 128 * h + 128] = out.astype(BF16)


def grad_body(place, att, c0, c_up, c_down, far_a, far_b, out, full, blocks):
    s = place[0]
    sides = []
    for step in (0, 3, 1, 2):
        row = pl.multiple_of(lax.rem(s + step, 4) * 128, 128)
        sides.append(att[pl.ds(row, 128), :])
    rhs = jnp.concatenate(sides, axis=0)
    for half, far in enumerate((far_a, far_b)):
        rows = slice(768 * half, 768 * half + 768)
        lhs = jnp.concatenate([c0[rows], c_up[rows], c_down[rows], far[...]], axis=1)
        full[rows] = jnp.dot(lhs, rhs, preferred_element_type=F32)
    for d in range(32):
        for z in range(4):
            blocks[48 * d + 12 * z : 48 * d + 12 * z + 12] = full[
                384 * z + 12 * d : 384 * z + 12 * d + 12
            ]
        out[d] = blocks[48 * d : 48 * d + 48].astype(BF16)


def moved(shard, axis, size, by, wrap):
    pairs = [(i, (i + by) % size) for i in range(size) if wrap or 0 <= i + by < size]
    return lax.ppermute(shard, axis, pairs)


def on_device(
    video,
    conv_weight,
    down_weight,
    noise,
    timesteps,
    embed_weight,
    mod_weight,
    qkv_weight,
    cotangent,
):
    core, zl, sec = lax.axis_index("core"), lax.axis_index("zl"), lax.axis_index("sec")
    above = moved(video[:, :, 127:128], "sec", 4, 1, False)
    below = moved(video[:, :, 0:1], "sec", 4, -1, False)
    v0 = jnp.concatenate([video, below, above], axis=2)
    v1 = moved(v0, SEQ, 128, 1, False)
    v2 = moved(v0, SEQ, 128, 2, False)

    cot = cotangent[0].T
    c_up = moved(cot, "sec", 4, 1, True)
    c_down = moved(cot, "sec", 4, -1, True)
    far_a = moved(c_up[0:768], "sec", 4, 1, True)
    far_b = moved(c_down[768:1536], "sec", 4, -1, True)

    stamps = lax.all_gather(timesteps, ("zl", "core"), axis=0, tiled=True).reshape(4, 2)
    mine = lax.dynamic_index_in_dim(stamps, core, 1, keepdims=False)
    theirs = lax.dynamic_index_in_dim(stamps, 1 - core, 1, keepdims=False)
    stamps = jnp.concatenate([mine, theirs])
    frequency = jnp.exp(-math.log(10000.0) * jnp.arange(128, dtype=F32) / 128)
    angles = stamps.astype(F32)[:, None] * frequency[None, :]
    temb = jnp.concatenate([jnp.cos(angles), jnp.sin(angles)], axis=1)
    place = jnp.stack([core, zl]).astype(jnp.int32)
    a_hi, a_lo, gram = call(
        prep_body,
        [
            jax.ShapeDtypeStruct((512, 384), BF16),
            jax.ShapeDtypeStruct((512, 384), BF16),
            jax.ShapeDtypeStruct((64, 64), F32),
        ],
        1,
        3,
        10**9,
        3 * 10**6,
    )(place, embed_weight, mod_weight, temb)
    rows = lax.all_gather(qkv_weight, ("x", "y"), axis=0, tiled=True)
    keep, send = call(
        fold_body,
        [jax.ShapeDtypeStruct((256, 1152), F32)] * 2,
        0,
        3,
        10**9,
        5 * 10**6,
    )(a_hi, a_lo, rows.transpose(1, 0, 2))
    pair = (keep + moved(send, "core", 2, 1, True)).astype(BF16).reshape(4, 64, 1152)
    parts = lax.all_to_all(pair, "zl", 0, 0, tiled=True)

    taps = conv_weight.reshape(128, 3, 3, 3, 3).transpose(0, 3, 4, 1, 2).reshape(128, 3, 27)
    taps = jnp.pad(taps, ((0, 0), (0, 0), (0, 5))).reshape(128, 96)
    conv = jnp.concatenate(
        [jnp.pad(taps, ((0, 0), (0, 32))), jnp.pad(taps, ((0, 0), (32, 0)))], axis=0
    )
    down = down_weight.transpose(1, 2, 3, 0).reshape(8, 128, 128)
    noise_t = noise.reshape(16, 8, 2, 16, 2).transpose(4, 2, 0, 1, 3).reshape(64, 128)
    level = (timesteps.astype(F32) + 1.0) / STEPS
    lat, pat = call(
        encode_body,
        [jax.ShapeDtypeStruct((256, 32), BF16), jax.ShapeDtypeStruct((64, 128), BF16)],
        1,
        6,
        10**10,
        10**6,
        [
            pltpu.VMEM((2, 4160, 128), F32),
            pltpu.VMEM((4160, 256), BF16),
            pltpu.VMEM((256, 256), BF16),
        ],
    )(level, v2, v1, v0, conv, down, noise_t)
    latents = lat.reshape(16, 16, 32).transpose(1, 0, 2)[:, None]

    pats = lax.all_gather(pat, "sec", axis=0)
    att = call(
        attend_body, jax.ShapeDtypeStruct((512, 384), BF16), 0, 3, 4 * 10**9, 10**6
    )(pats, parts, gram)
    attended = lax.all_to_all(att, "sec", split_axis=0, concat_axis=1, tiled=True)

    blocks = call(
        grad_body,
        jax.ShapeDtypeStruct((32, 48, 384), BF16),
        1,
        6,
        10**9,
        5 * 10**6,
        [pltpu.VMEM((1536, 384), F32), pltpu.VMEM((1536, 384), F32)],
    )(sec.astype(jnp.int32)[None], att, cot, c_up, c_down, far_a, far_b)
    got = lax.all_to_all(blocks, ("x", "y", "core"), 0, 0, tiled=True)
    summed = jnp.sum(got.astype(F32), axis=0).astype(BF16).reshape(4, 12, 384)
    last = lax.all_to_all(summed, "zl", 0, 0, tiled=True)
    out_grad = jnp.sum(last.astype(F32), axis=0)
    return (latents, attended[None], out_grad)


def solution(mesh):
    split = Mesh(mesh.devices.reshape(4, 4, 4, 4, 2), ("sec",) + SEQ)
    in_specs = (
        P(None, SEQ, "sec", None),
        P(),
        P(),
        P(None, SEQ, "sec", None),
        P(SEQ),
        P(),
        P(),
        P(SEQ, "sec", None),
        P(SEQ, "sec", None),
    )
    out_specs = (P(None, SEQ, "sec", None), P(SEQ, "sec", None), P(SEQ, "sec"))
    return jax.shard_map(
        on_device, mesh=split, in_specs=in_specs, out_specs=out_specs, check_vma=False
    )
```

time: 1730 us -> 236 us (0.14)
  waiting for transfers between devices: 1490 us -> 29.7 us
  local copies, waits for them, and re-layouts: 159 us -> 8.11 us
  blocking collectives: 0 us -> 91.6 us
  starting transfers between devices: 24.2 us -> 75.5 us
  matrix products: 30.4 us -> 0 us
  Pallas kernels: 0 us -> 26 us
    unnamed x5 -> x0, waiting for transfers between devices: 1250 us -> none
    all_gather x3 -> x0, waiting for transfers between devices: 212 us -> none  [the longest x1 119 us: on_device(): lax.all_gather(prepare(patches, embed_weight, mod_scale), 'sec', axis=0,...]
    unnamed x244 -> x19, local copies, waits for them, and re-layouts: 98.5 us -> 4.81 us
    all_gather x0 -> x2, blocking collectives: none -> 50.5 us  [the longest x1 29.6 us: on_device(): pats = lax.all_gather(pat, 'sec', axis=0)]
    another operation x2 -> x0, local copies, waits for them, and re-layouts: 48.3 us -> none  [encode_rows(): columns = jnp.stack(windows).reshape(len(windows), height * breadth)]
    ppermute x4 -> x9, starting transfers between devices: 16.7 us -> 50.7 us  [moved(): return lax.ppermute(shard, axis, pairs)]
    all_to_all x0 -> x1, blocking collectives: none -> 31.6 us  [on_device(): got = lax.all_to_all(blocks, ('x', 'y', 'core'), 0, 0, tiled=True)]
    dot_general x10 -> x0, matrix products: 30.4 us -> none  [the longest x1 8.22 us: on_device(): jnp.dot(grouped, weight_rows.reshape(weight_rows.shape[0], row_span), pre...]
  transfers between devices with their start and end apart: 9 -> 12, of which waited for: 7 -> 5; matrix products, arithmetic and copies ran while one was open for 11% -> 2% of each run, Pallas kernels for 0% -> 9%
where the time goes in v1:
time: 236 us; the launch traced here: 235 us
  blocking collectives  91.6 us (39%)
  starting transfers between devices  75.5 us (32%)
  waiting for transfers between devices  29.7 us (13%)
  Pallas kernels  26 us (11%)
  local copies, waits for them, and re-layouts  8.11 us (3%)
    ppermute x9, starting transfers between devices, moved(): return lax.ppermute(shard, axis, pairs)  50.7 us
    all_to_all x1, blocking collectives, on_device(): got = lax.all_to_all(blocks, ('x', 'y', 'core'), 0, 0, tiled=True)  31.6 us
    all_gather x1, blocking collectives, on_device(): pats = lax.all_gather(pat, 'sec', axis=0)  29.6 us
    all_gather x1, blocking collectives, on_device(): rows = lax.all_gather(qkv_weight, ('x', 'y'), axis=0, tiled=True)  20.9 us
    pallas_call x1, Pallas kernels, on_device(): call(encode_body, [jax.ShapeDtypeStruct((256, 32), BF16), jax.ShapeDtypeS...  16.8 us
    all_to_all x1, starting transfers between devices, on_device(): last = lax.all_to_all(summed, 'zl', 0, 0, tiled=True)  14.8 us
    all_to_all x1, waiting for transfers between devices, on_device(): lax.all_to_all(att, 'sec', split_axis=0, concat_axis=1, tiled=True)  14.3 us
    ppermute x9, waiting for transfers between devices, moved(): return lax.ppermute(shard, axis, pairs)  12.7 us
  transfers between devices with their start and end apart: 12, of which 5 were waited for; matrix products, arithmetic and copies ran while one was open for 2% of the time, Pallas kernels for 9%

profile of v1, /device:TPU:1, one launch (start us, length us, event | category | flops | bytes accessed | tf_op | source)
XLA Modules:
  0.0 234.7 jit_solution(16652040654347055053)
XLA Ops:
  3.3 9.5 %all-reduce.3 = s32[8]{0:T(128)S(1)} all-reduce(s32[8]{0:T(128)S(1)} %dynamic-update-slice), channel_id=1, replica_groups=mesh['sec'=4,'zl'=4,'x'=4,'y'=4,'core'=2] {'zl','core'}, use_global_device_ids=true, to_apply=%add.3 | all-reduce | flops 8 | bytes 64
  12.9 20.9 %all_gather.15 = bf16[384,3,384]{2,0,1:T(8,128)(2,1)S(1)} all-gather(bf16[24,3,384]{2,0,1:T(8,128)(2,1)} %param.16), channel_id=1, replica_groups=mesh['sec'=4,'zl'=4,'x'=4,'y'=4,'core'=2] {'x','y'}, dimensions={0}, use_global_device_ids=true | all-gather | bytes 940032 | tf_op jit(solution)/shard_map/all_gather | solution.py:250
  36.7 2.2 shard_map.113
  38.9 1.6 shard_map.114
  40.5 8.9 %collective-permute-start.4 = (f32[256,1152]{1,0:T(8,128)S(1)}, f32[256,1152]{1,0:T(8,128)S(1)}, u32[]{:S(2)}, u32[]{:S(2)}) collective-permute-start(f32[256,1152]{1,0:T(8,128)S(1)} %get-tuple-element.15), channel_id=1, source_target_pairs={{0,1},{1,0},{2,3},{3,2},{4,5},{5,4},{6,7},{7,6},{8,9},{9,8},{10,11... | collective-permute-start | bytes 3538952 | tf_op jit(solution)/shard_map/ppermute | solution.py:203
  49.5 2.5 %collective-permute-done.4 = f32[256,1152]{1,0:T(8,128)S(1)} collective-permute-done((f32[256,1152]{1,0:T(8,128)S(1)}, f32[256,1152]{1,0:T(8,128)S(1)}, u32[]{:S(2)}, u32[]{:S(2)}) %collective-permute-start.4) | collective-permute-done | bytes 1179680 | tf_op jit(solution)/shard_map/ppermute | solution.py:203
  52.9 3.6 %all-to-all-start = ((bf16[4,64,1152]{2,1,0:T(8,128)(2,1)}), bf16[4,64,1152]{2,1,0:T(8,128)(2,1)S(1)}, u32[]{:S(2)}, u32[]{:S(2)}) async-start(bf16[4,64,1152]{2,1,0:T(8,128)(2,1)} %bitcast.14), calls=%async_computation | async-start | bytes 1179648 | tf_op jit(solution)/shard_map/all_to_all | solution.py:260
  58.0 9.4 %collective-permute-start.1 = (bf16[3,1,1,256]{3,2,1,0:T(2,128)(2,1)S(1)}, bf16[3,1,1,256]{3,2,1,0:T(2,128)(2,1)S(1)}, u32[]{:S(2)}, u32[]{:S(2)}) collective-permute-start(bf16[3,1,1,256]{3,2,1,0:T(2,128)(2,1)S(1)} %get-tuple-element.20), channel_id=1, source_target_pairs={{0,128},{128,256},{256,384},{1,129},{129,257},{257,385},{2,130},{1... | collective-permute-start | bytes 4616 | tf_op jit(solution)/shard_map/ppermute | solution.py:203
  68.2 2.8 %collective-permute-start.2 = (bf16[3,1,130,256]{3,2,1,0:T(8,128)(2,1)S(1)}, bf16[3,1,130,256]{3,2,1,0:T(8,128)(2,1)S(1)}, u32[]{:S(2)}, u32[]{:S(2)}) collective-permute-start(bf16[3,1,130,256]{3,2,1,0:T(8,128)(2,1)S(1)} %pad_maximum_fusion.v0), channel_id=1, source_target_pairs={{0,2},{1,3},{2,4},{3,5},{4,6},{5,7},{6,8},{7,9},{8,10},{9,11},{10,... | collective-permute-start | bytes 599048 | tf_op jit(solution)/shard_map/ppermute | solution.py:203
  71.0 4.3 %collective-permute-start.3 = (bf16[3,1,130,256]{3,2,1,0:T(8,128)(2,1)S(1)}, bf16[3,1,130,256]{3,2,1,0:T(8,128)(2,1)S(1)}, u32[]{:S(2)}, u32[]{:S(2)}) collective-permute-start(bf16[3,1,130,256]{3,2,1,0:T(8,128)(2,1)S(1)} %pad_maximum_fusion.v0), channel_id=1, source_target_pairs={{0,1},{1,2},{2,3},{3,4},{4,5},{5,6},{6,7},{7,8},{8,9},{9,10},{10,1... | collective-permute-start | bytes 599048 | tf_op jit(solution)/shard_map/ppermute | solution.py:203
  75.5 7.9 %collective-permute-start.5 = (bf16[1536,128]{1,0:T(8,128)(2,1)S(1)}, bf16[1536,128]{1,0:T(8,128)(2,1)S(1)}, u32[]{:S(2)}, u32[]{:S(2)}) collective-permute-start(bf16[1536,128]{1,0:T(8,128)(2,1)S(1)} %bitcast.35), channel_id=1, source_target_pairs={{0,128},{128,256},{256,384},{384,0},{1,129},{129,257},{257,385},{3... | collective-permute-start | bytes 1179656 | tf_op jit(solution)/shard_map/ppermute | solution.py:203
  83.5 6.4 %collective-permute-start.6 = (bf16[1536,128]{1,0:T(8,128)(2,1)S(1)}, bf16[1536,128]{1,0:T(8,128)(2,1)S(1)}, u32[]{:S(2)}, u32[]{:S(2)}) collective-permute-start(bf16[1536,128]{1,0:T(8,128)(2,1)S(1)} %bitcast.36), channel_id=1, source_target_pairs={{0,384},{128,0},{256,128},{384,256},{1,385},{129,1},{257,129},{385... | collective-permute-start | bytes 1179656 | tf_op jit(solution)/shard_map/ppermute | solution.py:203
  90.7 16.8 %shard_map.112 = (bf16[256,32]{1,0:T(8,128)(2,1)S(1)}, bf16[64,128]{1,0:T(8,128)(2,1)S(1)}) custom-call(f32[1]{0:T(128)S(6)} %div.9.level, bf16[3,1,130,256]{3,2,1,0:T(8,128)(2,1)S(1)} %collective-permute-done.2.v2, bf16[3,1,130,256]{3,2,1,0:T(8,128)(2,1)S(1)} %collective-permute-done.3.v1, bf16[3,1,130,256]{3,2,1,0:T(8,128)(2,1)S(1)} %pad_maximum_fusion.v0, ...), custom_call_target="tpu_custom_call" | custom-call | flops 10000000000 | bytes 1000000 | tf_op jit(solution)/shard_map/pallas_call | solution.py:270
  107.6 29.6 %all-gather = bf16[256,128]{1,0:T(8,128)(2,1)S(1)} all-gather(bf16[64,128]{1,0:T(8,128)(2,1)S(1)} %get-tuple-element.11), channel_id=2, replica_groups=mesh['sec'=4,'zl'=4,'x'=4,'y'=4,'core'=2] {'sec'}, dimensions={0}, use_global_device_ids=true | all-gather | bytes 81920 | tf_op jit(solution)/shard_map/all_gather | solution.py:285
  137.2 6.2 %collective-permute-start.7 = (bf16[768,128]{1,0:T(8,128)(2,1)S(1)}, bf16[768,128]{1,0:T(8,128)(2,1)S(1)}, u32[]{:S(2)}, u32[]{:S(2)}) collective-permute-start(bf16[768,128]{1,0:T(8,128)(2,1)S(1)} %slice.16), channel_id=1, source_target_pairs={{0,128},{128,256},{256,384},{384,0},{1,129},{129,257},{257,385},{3... | collective-permute-start | bytes 589832 | tf_op jit(solution)/shard_map/ppermute | solution.py:203
  143.5 3.1 %collective-permute-start.8 = (bf16[768,128]{1,0:T(8,128)(2,1)S(1)}, bf16[768,128]{1,0:T(8,128)(2,1)S(1)}, u32[]{:S(2)}, u32[]{:S(2)}) collective-permute-start(bf16[768,128]{1,0:T(8,128)(2,1)S(1)} %slice.17), channel_id=1, source_target_pairs={{0,384},{128,0},{256,128},{384,256},{1,385},{129,1},{257,129},{385... | collective-permute-start | bytes 589832 | tf_op jit(solution)/shard_map/ppermute | solution.py:203
  146.6 3.3 %shard_map.115.att = bf16[512,384]{1,0:T(8,128)(2,1)} custom-call(bf16[4,64,128]{2,1,0:T(8,128)(2,1)S(1)} %bitcast.38, bf16[4,64,1152]{2,1,0:T(8,128)(2,1)S(1)} %all-to-all-done.parts, f32[64,64]{1,0:T(8,128)S(1)} %get-tuple-element.16.gram), custom_call_target="tpu_custom_call" | custom-call | flops 4000000000 | bytes 1000000 | tf_op jit(solution)/shard_map/pallas_call | solution.py:286
  149.9 9.5 %collective-permute-done.8.far_b = bf16[768,128]{1,0:T(8,128)(2,1)S(1)} collective-permute-done((bf16[768,128]{1,0:T(8,128)(2,1)S(1)}, bf16[768,128]{1,0:T(8,128)(2,1)S(1)}, u32[]{:S(2)}, u32[]{:S(2)}) %collective-permute-start.8) | collective-permute-done | bytes 196640 | tf_op jit(solution)/shard_map/ppermute | solution.py:203
  159.4 2.1 shard_map.116
  161.6 31.6 %all_to_all.31 = bf16[32,48,384]{2,1,0:T(8,128)(2,1)S(1)} all-to-all(bf16[32,48,384]{2,1,0:T(8,128)(2,1)S(1)} %shard_map.116), channel_id=1, replica_groups=mesh['sec'=4,'zl'=4,'x'=4,'y'=4,'core'=2] {'x','y','core'}, dimensions={0} | all-to-all | bytes 2359296 | tf_op jit(solution)/shard_map/all_to_all | solution.py:300
  193.2 6.4 %all-to-all-start.1 = ((bf16[4,128,384]{2,1,0:T(8,128)(2,1)}), bf16[4,128,384]{2,1,0:T(8,128)(2,1)S(1)}, u32[]{:S(2)}, u32[]{:S(2)}) async-start(bf16[4,128,384]{2,1,0:T(8,128)(2,1)} %bitcast.15), calls=%async_computation.1 | async-start | bytes 786432 | tf_op jit(solution)/shard_map/all_to_all | solution.py:289
  200.4 14.3 %all-to-all-done.1 = bf16[4,128,384]{2,1,0:T(8,128)(2,1)S(1)} async-done(((bf16[4,128,384]{2,1,0:T(8,128)(2,1)}), bf16[4,128,384]{2,1,0:T(8,128)(2,1)S(1)}, u32[]{:S(2)}, u32[]{:S(2)}) %all-to-all-start.1) | async-done | bytes 393248 | tf_op jit(solution)/shard_map/all_to_all | solution.py:289
  214.7 14.8 %all-to-all-start.3 = ((bf16[4,12,384]{2,1,0:T(8,128)(2,1)}), bf16[4,12,384]{2,1,0:T(8,128)(2,1)S(1)}, u32[]{:S(2)}, u32[]{:S(2)}) async-start(bf16[4,12,384]{2,1,0:T(8,128)(2,1)} %reshape.69), calls=%async_computation.3 | async-start | bytes 98304 | tf_op jit(solution)/shard_map/all_to_all | solution.py:302
  231.4 2.7 %all-to-all-done.3 = bf16[4,12,384]{2,1,0:T(8,128)(2,1)S(1)} async-done(((bf16[4,12,384]{2,1,0:T(8,128)(2,1)}), bf16[4,12,384]{2,1,0:T(8,128)(2,1)S(1)}, u32[]{:S(2)}, u32[]{:S(2)}) %all-to-all-start.3) | async-done | bytes 36896 | tf_op jit(solution)/shard_map/all_to_all | solution.py:302
  (54 shorter events, 12.4 us)
Async XLA Ops:
  34.3 1.4 copy-start
  35.8 1.0 copy-start.1
  40.5 11.4 %collective-permute-start.4 = (f32[256,1152]{1,0:T(8,128)S(1)}, f32[256,1152]{1,0:T(8,128)S(1)}, u32[]{:S(2)}, u32[]{:S(2)}) collective-permute-start(f32[256,1152]{1,0:T(8,128)S(1)} %get-tuple-element.15), channel_id=1, source_target_pairs={{0,1},{1,0},{2,3},{3,2},{4,5},{5,4},{6,7},{7,6},{8,9},{9,8},{10,11... | collective-permute-start | bytes 3538952 | tf_op jit(solution)/shard_map/ppermute | solution.py:203
  52.9 3.6 %copy-start.4 = (bf16[3,1,128,256]{3,2,1,0:T(8,128)(2,1)S(1)}, bf16[3,1,128,256]{3,2,1,0:T(8,128)(2,1)}, u32[]{:S(2)}) copy-start(bf16[3,1,128,256]{3,2,1,0:T(8,128)(2,1)} %param.9) | copy-start | bytes 589828
  52.9 22.4 %copy-start.3 = (bf16[1,128,1536]{2,1,0:T(8,128)(2,1)S(1)}, bf16[1,128,1536]{2,1,0:T(8,128)(2,1)}, u32[]{:S(2)}) copy-start(bf16[1,128,1536]{2,1,0:T(8,128)(2,1)} %param.17) | copy-start | bytes 1179652
  52.9 37.0 %copy-start.5 = (bf16[16,1,16,32]{3,2,1,0:T(8,128)(2,1)S(1)}, bf16[16,1,16,32]{3,2,1,0:T(8,128)(2,1)}, u32[]{:S(2)}) copy-start(bf16[16,1,16,32]{3,2,1,0:T(8,128)(2,1)} %param.12) | copy-start | bytes 49156
  52.9 93.7 %all-to-all-start = ((bf16[4,64,1152]{2,1,0:T(8,128)(2,1)}), bf16[4,64,1152]{2,1,0:T(8,128)(2,1)S(1)}, u32[]{:S(2)}, u32[]{:S(2)}) async-start(bf16[4,64,1152]{2,1,0:T(8,128)(2,1)} %bitcast.14), calls=%async_computation | async-start | bytes 1179648 | tf_op jit(solution)/shard_map/all_to_all | solution.py:260
  56.5 33.9 %copy-start.6 = (bf16[128,81]{0,1:T(8,128)(2,1)S(1)}, bf16[128,81]{0,1:T(8,128)(2,1)}, u32[]{:S(2)}) copy-start(bf16[128,81]{0,1:T(8,128)(2,1)} %param.10) | copy-start | bytes 62212
  56.5 34.2 %copy-start.2 = (bf16[128,8,8,16]{0,3,2,1:T(8,128)(2,1)S(1)}, bf16[128,8,8,16]{0,3,2,1:T(8,128)(2,1)}, u32[]{:S(2)}) copy-start(bf16[128,8,8,16]{0,3,2,1:T(8,128)(2,1)} %param.11) | copy-start | bytes 786436
  56.5 10.9 %collective-permute-start = (bf16[3,1,1,256]{3,2,1,0:T(2,128)(2,1)S(1)}, bf16[3,1,1,256]{3,2,1,0:T(2,128)(2,1)S(1)}, u32[]{:S(2)}, u32[]{:S(2)}) collective-permute-start(bf16[3,1,1,256]{3,2,1,0:T(2,128)(2,1)S(1)} %get-tuple-element.19), channel_id=1, source_target_pairs={{128,0},{256,128},{384,256},{129,1},{257,129},{385,257},{130,2},{2... | collective-permute-start | bytes 4616 | tf_op jit(solution)/shard_map/ppermute | solution.py:203
  58.0 10.2 %collective-permute-start.1 = (bf16[3,1,1,256]{3,2,1,0:T(2,128)(2,1)S(1)}, bf16[3,1,1,256]{3,2,1,0:T(2,128)(2,1)S(1)}, u32[]{:S(2)}, u32[]{:S(2)}) collective-permute-start(bf16[3,1,1,256]{3,2,1,0:T(2,128)(2,1)S(1)} %get-tuple-element.20), channel_id=1, source_target_pairs={{0,128},{128,256},{256,384},{1,129},{129,257},{257,385},{2,130},{1... | collective-permute-start | bytes 4616 | tf_op jit(solution)/shard_map/ppermute | solution.py:203
  68.2 22.5 %collective-permute-start.2 = (bf16[3,1,130,256]{3,2,1,0:T(8,128)(2,1)S(1)}, bf16[3,1,130,256]{3,2,1,0:T(8,128)(2,1)S(1)}, u32[]{:S(2)}, u32[]{:S(2)}) collective-permute-start(bf16[3,1,130,256]{3,2,1,0:T(8,128)(2,1)S(1)} %pad_maximum_fusion.v0), channel_id=1, source_target_pairs={{0,2},{1,3},{2,4},{3,5},{4,6},{5,7},{6,8},{7,9},{8,10},{9,11},{10,... | collective-permute-start | bytes 599048 | tf_op jit(solution)/shard_map/ppermute | solution.py:203
  71.0 19.7 %collective-permute-start.3 = (bf16[3,1,130,256]{3,2,1,0:T(8,128)(2,1)S(1)}, bf16[3,1,130,256]{3,2,1,0:T(8,128)(2,1)S(1)}, u32[]{:S(2)}, u32[]{:S(2)}) collective-permute-start(bf16[3,1,130,256]{3,2,1,0:T(8,128)(2,1)S(1)} %pad_maximum_fusion.v0), channel_id=1, source_target_pairs={{0,1},{1,2},{2,3},{3,4},{4,5},{5,6},{6,7},{7,8},{8,9},{9,10},{10,1... | collective-permute-start | bytes 599048 | tf_op jit(solution)/shard_map/ppermute | solution.py:203
  75.5 61.6 %collective-permute-start.5 = (bf16[1536,128]{1,0:T(8,128)(2,1)S(1)}, bf16[1536,128]{1,0:T(8,128)(2,1)S(1)}, u32[]{:S(2)}, u32[]{:S(2)}) collective-permute-start(bf16[1536,128]{1,0:T(8,128)(2,1)S(1)} %bitcast.35), channel_id=1, source_target_pairs={{0,128},{128,256},{256,384},{384,0},{1,129},{129,257},{257,385},{3... | collective-permute-start | bytes 1179656 | tf_op jit(solution)/shard_map/ppermute | solution.py:203
  83.5 59.9 %collective-permute-start.6 = (bf16[1536,128]{1,0:T(8,128)(2,1)S(1)}, bf16[1536,128]{1,0:T(8,128)(2,1)S(1)}, u32[]{:S(2)}, u32[]{:S(2)}) collective-permute-start(bf16[1536,128]{1,0:T(8,128)(2,1)S(1)} %bitcast.36), channel_id=1, source_target_pairs={{0,384},{128,0},{256,128},{384,256},{1,385},{129,1},{257,129},{385... | collective-permute-start | bytes 1179656 | tf_op jit(solution)/shard_map/ppermute | solution.py:203
  137.2 12.7 %collective-permute-start.7 = (bf16[768,128]{1,0:T(8,128)(2,1)S(1)}, bf16[768,128]{1,0:T(8,128)(2,1)S(1)}, u32[]{:S(2)}, u32[]{:S(2)}) collective-permute-start(bf16[768,128]{1,0:T(8,128)(2,1)S(1)} %slice.16), channel_id=1, source_target_pairs={{0,128},{128,256},{256,384},{384,0},{1,129},{129,257},{257,385},{3... | collective-permute-start | bytes 589832 | tf_op jit(solution)/shard_map/ppermute | solution.py:203
  143.5 16.0 %collective-permute-start.8 = (bf16[768,128]{1,0:T(8,128)(2,1)S(1)}, bf16[768,128]{1,0:T(8,128)(2,1)S(1)}, u32[]{:S(2)}, u32[]{:S(2)}) collective-permute-start(bf16[768,128]{1,0:T(8,128)(2,1)S(1)} %slice.17), channel_id=1, source_target_pairs={{0,384},{128,0},{256,128},{384,256},{1,385},{129,1},{257,129},{385... | collective-permute-start | bytes 589832 | tf_op jit(solution)/shard_map/ppermute | solution.py:203
  193.2 21.5 %all-to-all-start.1 = ((bf16[4,128,384]{2,1,0:T(8,128)(2,1)}), bf16[4,128,384]{2,1,0:T(8,128)(2,1)S(1)}, u32[]{:S(2)}, u32[]{:S(2)}) async-start(bf16[4,128,384]{2,1,0:T(8,128)(2,1)} %bitcast.15), calls=%async_computation.1 | async-start | bytes 786432 | tf_op jit(solution)/shard_map/all_to_all | solution.py:289
  214.7 19.4 %all-to-all-start.3 = ((bf16[4,12,384]{2,1,0:T(8,128)(2,1)}), bf16[4,12,384]{2,1,0:T(8,128)(2,1)S(1)}, u32[]{:S(2)}, u32[]{:S(2)}) async-start(bf16[4,12,384]{2,1,0:T(8,128)(2,1)} %reshape.69), calls=%async_computation.3 | async-start | bytes 98304 | tf_op jit(solution)/shard_map/all_to_all | solution.py:302

commit v2 on v1

v2 whole, which is shorter than its diff:
```python
import math

import jax
import jax.numpy as jnp
from jax import lax
from jax.experimental import pallas as pl
from jax.experimental.pallas import tpu as pltpu
from jax.sharding import Mesh, PartitionSpec as P

STEPS = 1000
SEQ = ("zl", "x", "y", "core")
F32 = jnp.float32
BF16 = jnp.bfloat16
VMEM = pl.BlockSpec(memory_space=pltpu.VMEM)
SMEM = pl.BlockSpec(memory_space=pltpu.SMEM)
ANY = pl.BlockSpec(memory_space=pl.ANY)
VMEM_BYTES = 48 * 1024 * 1024


def call(body, out_shape, n_smem, n_vmem, flops, nbytes, scratch=(), n_any=0):
    several = isinstance(out_shape, (list, tuple))
    return pl.pallas_call(
        body,
        out_shape=out_shape,
        in_specs=[SMEM] * n_smem + [VMEM] * n_vmem + [ANY] * n_any,
        out_specs=[VMEM] * len(out_shape) if several else VMEM,
        scratch_shapes=list(scratch),
        compiler_params=pltpu.CompilerParams(vmem_limit_bytes=VMEM_BYTES),
        cost_estimate=pl.CostEstimate(flops=flops, bytes_accessed=nbytes, transcendentals=0),
    )


def iota(shape, dim):
    return lax.broadcasted_iota(jnp.int32, shape, dim)


def one_hot(where):
    return jnp.where(where, 1.0, 0.0).astype(BF16)


def prep_body(place, embed, mod, temb, a_hi, a_lo, gram):
    to, of = iota((64, 64), 0), iota((64, 64), 1)
    order = one_hot(of == (to & 15) * 4 + ((to >> 4) & 1) * 2 + (to >> 5))
    emb = jnp.dot(order, embed[...], preferred_element_type=F32)
    mean = jnp.mean(emb, axis=1, keepdims=True)
    center = emb - mean
    gram[...] = (
        lax.dot_general(
            center,
            center,
            (((1,), (1,)), ((), ())),
            precision=lax.Precision.HIGHEST,
            preferred_element_type=F32,
        )
        / embed.shape[1]
    )
    col = iota((768, 192), 1)
    part = (col * 1366) >> 16
    hit = iota((768, 192), 0) == 48 * place[0] + col - 48 * part
    emb16 = emb.astype(BF16)
    emb_pick = jnp.zeros((64, 192), F32)
    mod_pick = jnp.zeros((256, 192), F32)
    for z in range(4):
        pick = one_hot(hit & (part == z))
        at = slice(768 * z, 768 * z + 768)
        emb_pick = emb_pick + jnp.dot(emb16[:, at], pick, preferred_element_type=F32)
        mod_pick = mod_pick + jnp.dot(mod[:, at], pick, preferred_element_type=F32)
    emb_pick = emb_pick - mean
    t = temb[...]
    first = t.astype(BF16).astype(F32)
    second = (t - first).astype(BF16).astype(F32)
    third = t - first - second
    pieces = jnp.concatenate([first, second, third], axis=0).astype(BF16)
    scale = jnp.dot(pieces, mod_pick.astype(BF16), preferred_element_type=F32)
    scale = 1.0 + (scale[0:16] + scale[16:32] + scale[32:48])
    for f in range(16):
        a = emb_pick * scale[f : f + 1]
        hi = a.astype(BF16)
        a_hi[64 * f : 64 * f + 64] = hi
        a_lo[64 * f : 64 * f + 64] = (a - hi.astype(F32)).astype(BF16)


def fold_body(a_hi, a_lo, w, out):
    for h in range(3):
        prod = jnp.dot(a_hi[...], w[h], preferred_element_type=F32) + jnp.dot(
            a_lo[...], w[h], preferred_element_type=F32
        )
        out[:, 384 * h : 384 * h + 384] = prod.astype(BF16)


def encode_body(
    level, v2, v1, v0, conv, down, noise, lat, pat, s32, edge, s16, rows_out
):
    x = iota((136, 256), 1)
    for c in range(3):
        for dt, v in enumerate((v2, v1, v0)):
            img = v[c, 0].astype(F32)
            left = jnp.where(x[:130] == 0, 0.0, pltpu.roll(img, 1, 1))
            right = jnp.where(x[:130] == 255, 0.0, pltpu.roll(img, 255, 1))
            for dx, shifted in enumerate((left, img, right)):
                k = dx * 9 + c * 3 + dt
                s32[k] = shifted[0:128]
                edge[k : k + 1] = shifted[128:129]
                edge[32 + k : 33 + k] = shifted[129:130]
    s32[27:32] = jnp.zeros((5, 128, 256), F32)
    edge[27:32] = jnp.zeros((5, 256), F32)
    edge[59:64] = jnp.zeros((5, 256), F32)
    s16[0:32] = edge[0:32].astype(BF16)
    s16[4128:4160] = edge[32:64].astype(BF16)
    for y in range(0, 128, 8):
        taps = jnp.swapaxes(s32[:, y : y + 8, :], 0, 1).reshape(256, 256)
        s16[32 * y + 32 : 32 * y + 288] = taps.astype(BF16)
    own_lane = (iota((128, 256), 1) & 7) == (iota((128, 256), 0) >> 4)

    def block_row(a, _):
        feats = []
        for q in range(4):
            taps = s16[pl.ds(pl.multiple_of(a * 256 + 64 * q, 64), 128), :]
            pre = jnp.dot(conv[...], taps, preferred_element_type=F32)
            half = 0.5 * pre
            feats.append((half + half * jnp.tanh(half)).astype(BF16))
        feature = jnp.concatenate(feats, axis=0)
        weights = jnp.concatenate([down[i] for i in range(8)], axis=1)
        prod = jnp.dot(weights, feature, preferred_element_type=F32)
        prod = jnp.where(own_lane, prod, 0.0)
        acc = prod[0:16]
        for j in range(1, 8):
            acc = acc + prod[16 * j : 16 * j + 16]
        for by in (1, 2, 4):
            acc = acc + pltpu.roll(acc, 256 - by, 1)
        rows_out[pl.ds(pl.multiple_of(a * 16, 16), 16), :] = acc.astype(BF16)
        return 0

    lax.fori_loop(0, 16, block_row, 0, unroll=True)
    pick = one_hot(iota((256, 32), 0) == 8 * iota((256, 32), 1))
    lat[...] = jnp.dot(rows_out[...], pick, preferred_element_type=F32).astype(BF16)
    px, tok = iota((256, 128), 0), iota((256, 128), 1)
    for w in range(2):
        acc = jnp.zeros((32, 128), F32)
        for r in range(8):
            place = one_hot((px == 16 * (tok & 15) + 8 * w) & ((tok >> 4) == r))
            acc = acc + jnp.dot(
                rows_out[32 * r : 32 * r + 32], place, preferred_element_type=F32
            )
        t = level[0]
        mixed = (1.0 - t) * acc + t * noise[32 * w : 32 * w + 32].astype(F32)
        pat[32 * w : 32 * w + 32] = mixed.astype(BF16)


def attend_body(pats, parts, gram, att):
    tokens_t = jnp.concatenate([pats[s] for s in range(4)], axis=1).astype(F32)
    tokens = tokens_t.T
    spread = jnp.sum(
        tokens
        * jnp.dot(
            tokens, gram[...], precision=lax.Precision.HIGHEST, preferred_element_type=F32
        ),
        axis=1,
        keepdims=True,
    )
    scale = lax.rsqrt(spread + 1e-06)
    total = parts[0].astype(F32)
    for i in range(1, 16):
        total = total + parts[i].astype(F32)
    hi = total.astype(BF16)
    lo = (total - hi.astype(F32)).astype(BF16)
    weights = jnp.concatenate([hi, lo], axis=0)
    twice = jnp.concatenate([tokens, tokens], axis=1).astype(BF16)
    for h in range(3):
        proj = jnp.dot(
            twice, weights[:, 384 * h : 384 * h + 384], preferred_element_type=F32
        )
        proj = (proj * scale).astype(BF16)
        q, k, v = proj[:, 0:128], proj[:, 128:256], proj[:, 256:384]
        scores = lax.dot_general(
            q, k, (((1,), (1,)), ((), ())), preferred_element_type=F32
        ) * (1.0 / math.sqrt(128.0))
        probs = jnp.exp(scores - jnp.max(scores, axis=1, keepdims=True))
        norm = 1.0 / jnp.sum(probs, axis=1, keepdims=True)
        out = jnp.dot(probs.astype(BF16), v, preferred_element_type=F32) * norm
        att[:, 128 * h : 128 * h + 128] = out.astype(BF16)


def grad_body(place, att, c0, c_up, c_down, far_a, far_b, out0, out1, out2, out3, full):
    sec, y = place[0], place[1]
    sides = []
    for step in (0, 3, 1, 2):
        row = pl.multiple_of(((sec + step) & 3) * 128, 128)
        sides.append(att[pl.ds(row, 128), :])
    rhs = jnp.concatenate(sides, axis=0)
    for half, far in enumerate((far_a, far_b)):
        rows = slice(768 * half, 768 * half + 768)
        lhs = jnp.concatenate([c0[rows], c_up[rows], c_down[rows], far[...]], axis=1)
        full[rows] = jnp.dot(lhs, rhs, preferred_element_type=F32)
    for by, out in enumerate((out0, out1, out2, out3)):
        to_y = (y + by) & 3
        for zx in range(0, 16, 2):
            pair = [
                full[pl.ds(pl.multiple_of(24 * to_y + 96 * k, 8), 24), :] for k in (zx, zx + 1)
            ]
            out[24 * zx : 24 * zx + 48] = jnp.concatenate(pair, axis=0).astype(BF16)


def gate_body(value, *rest):
    rest[-1][...] = value[...]


def gated(value, *deps):
    return pl.pallas_call(
        gate_body,
        out_shape=jax.ShapeDtypeStruct(value.shape, value.dtype),
        in_specs=[VMEM] + [ANY] * len(deps),
        out_specs=VMEM,
    )(value, *deps)


def together(*values):
    return lax.optimization_barrier(values)


def moved(shard, axis, size, by, wrap):
    pairs = [(i, (i + by) % size) for i in range(size) if wrap or 0 <= i + by < size]
    return lax.ppermute(shard, axis, pairs)


def on_device(
    video,
    conv_weight,
    down_weight,
    noise,
    timesteps,
    embed_weight,
    mod_weight,
    qkv_weight,
    cotangent,
):
    above = moved(video[:, :, 127:128], ("sec",), 4, 1, False)
    below = moved(video[:, :, 0:1], ("sec",), 4, -1, False)
    v0 = jnp.concatenate([video, above, below], axis=2)
    v1, v2 = moved(v0, SEQ, 128, 1, False), moved(v0, SEQ, 128, 2, False)

    rows = lax.all_to_all(
        jnp.broadcast_to(qkv_weight.transpose(1, 0, 2), (8, 3, 24, 384)), ("zl", "core"), 0, 0, tiled=True
    )
    rows = rows.transpose(1, 0, 2, 3).reshape(3, 192, 384)
    stamps = lax.all_gather(gated(timesteps, v1, v2), ("x", "y"), axis=0, tiled=True)

    cot = gated(cotangent[0].T, above, below)
    c_up = moved(cot, "sec", 4, 1, True)
    c_down = moved(cot, "sec", 4, -1, True)

    frequency = jnp.exp(-math.log(10000.0) * jnp.arange(128, dtype=F32) / 128)
    angles = stamps.astype(F32)[:, None] * frequency[None, :]
    temb = jnp.concatenate([jnp.cos(angles), jnp.sin(angles)], axis=1)
    place = (lax.axis_index("x") * 4 + lax.axis_index("y")).astype(jnp.int32)[None]
    a_hi, a_lo, gram = call(
        prep_body,
        [
            jax.ShapeDtypeStruct((1024, 192), BF16),
            jax.ShapeDtypeStruct((1024, 192), BF16),
            jax.ShapeDtypeStruct((64, 64), F32),
        ],
        1,
        3,
        10**9,
        3 * 10**6,
    )(place, embed_weight, mod_weight, temb)
    partial = call(
        fold_body, jax.ShapeDtypeStruct((1024, 1152), BF16), 0, 3, 10**9, 5 * 10**6
    )(a_hi, a_lo, rows)
    taps = conv_weight.reshape(128, 3, 3, 3, 3).transpose(0, 3, 4, 1, 2).reshape(128, 3, 27)
    taps = jnp.pad(taps, ((0, 0), (0, 0), (0, 5))).reshape(128, 96)
    conv = jnp.concatenate(
        [jnp.pad(taps, ((0, 0), (0, 32))), jnp.pad(taps, ((0, 0), (32, 0)))], axis=0
    )
    down = down_weight.transpose(1, 2, 3, 0).reshape(8, 128, 128)
    noise_t = noise.reshape(16, 8, 2, 16, 2).transpose(4, 2, 0, 1, 3).reshape(64, 128)
    level = (timesteps.astype(F32) + 1.0) / STEPS
    lat, pat = call(
        encode_body,
        [jax.ShapeDtypeStruct((256, 32), BF16), jax.ShapeDtypeStruct((64, 128), BF16)],
        1,
        6,
        10**10,
        10**6,
        [
            pltpu.VMEM((32, 128, 256), F32),
            pltpu.VMEM((64, 256), F32),
            pltpu.VMEM((4160, 256), BF16),
            pltpu.VMEM((256, 256), BF16),
        ],
    )(level, v2, v1, v0, conv, down, noise_t)
    latents = lat.reshape(16, 16, 32).transpose(1, 0, 2)[:, None]

    pat, partial, c_up, c_down = together(pat, partial, c_up, c_down)
    parts = lax.all_to_all(partial.reshape(16, 64, 1152), ("x", "y"), 0, 0, tiled=True)
    pats = lax.all_gather(pat, "sec", axis=0)
    pats, c_up, c_down = together(pats, c_up, c_down)
    far_a = moved(c_up[0:768], "sec", 4, 1, True)
    far_b = moved(c_down[768:1536], "sec", 4, -1, True)
    parts, far_a, far_b = together(parts, far_a, far_b)
    att = call(
        attend_body, jax.ShapeDtypeStruct((512, 384), BF16), 0, 3, 4 * 10**9, 10**6
    )(pats, parts, gram)
    attended = lax.all_to_all(att, "sec", split_axis=0, concat_axis=1, tiled=True)

    sums = call(
        grad_body,
        [jax.ShapeDtypeStruct((384, 384), BF16)] * 4,
        1,
        6,
        10**9,
        5 * 10**6,
        [pltpu.VMEM((1536, 384), F32)],
    )(
        jnp.stack([lax.axis_index("sec"), lax.axis_index("y")]).astype(jnp.int32),
        att,
        cot,
        c_up,
        c_down,
        far_a,
        far_b,
    )
    got = [moved(sums[by], "y", 4, by, True).astype(F32) for by in range(1, 4)]
    column = sum(got, sums[0].astype(F32)).astype(BF16).reshape(32, 12, 384)
    last = lax.all_to_all(column, ("zl", "x", "core"), 0, 0, tiled=True)
    out_grad = jnp.sum(last.astype(F32), axis=0)
    return (latents, attended[None], out_grad)


def solution(mesh):
    split = Mesh(mesh.devices.reshape(4, 4, 4, 4, 2), ("sec",) + SEQ)
    in_specs = (
        P(None, SEQ, "sec", None),
        P(),
        P(),
        P(None, SEQ, "sec", None),
        P(SEQ),
        P(),
        P(),
        P(SEQ, "sec", None),
        P(SEQ, "sec", None),
    )
    out_specs = (P(None, SEQ, "sec", None), P(SEQ, "sec", None), P(SEQ, "sec"))
    return jax.shard_map(
        on_device, mesh=split, in_specs=in_specs, out_specs=out_specs, check_vma=False
    )
```

time: 236 us -> 195 us (0.83)
  blocking collectives: 91.6 us -> 33.4 us
  starting transfers between devices: 75.5 us -> 95.9 us
  local copies, waits for them, and re-layouts: 8.11 us -> 19.8 us
  waiting for transfers between devices: 29.7 us -> 22.2 us
  Pallas kernels: 26 us -> 19.6 us
    all_to_all x1 -> x0, blocking collectives: 31.6 us -> none  [on_device(): got = lax.all_to_all(blocks, ('x', 'y', 'core'), 0, 0, tiled=True)]
    all_to_all x2 -> x3, starting transfers between devices: 18.5 us -> 40.8 us  [the longest x1 27.9 us: on_device(): last = lax.all_to_all(column, ('zl', 'x', 'core'), 0, 0, tiled=True)]
    all_gather x1 -> x0, blocking collectives: 20.9 us -> none  [on_device(): rows = lax.all_gather(qkv_weight, ('x', 'y'), axis=0, tiled=True)]
    all_to_all x1, waiting for transfers between devices: 14.3 us -> 0.01 us  [on_device(): lax.all_to_all(att, 'sec', split_axis=0, concat_axis=1, tiled=True)]
    pallas_call x1, Pallas kernels: 16.8 us -> 6.43 us  [on_device(): call(encode_body, [jax.ShapeDtypeStruct((256, 32), BF16), jax.ShapeDtypeS...]
    all_gather x1, blocking collectives: 29.6 us -> 19.7 us  [on_device(): pats = lax.all_gather(pat, 'sec', axis=0)]
    all_to_all x2 -> x3, waiting for transfers between devices: 2.7 us -> 11.9 us  [the longest x1 11.9 us: on_device(): last = lax.all_to_all(column, ('zl', 'x', 'core'), 0, 0, tiled=True)]
    unnamed x19 -> x47, local copies, waits for them, and re-layouts: 4.81 us -> 13.4 us
  transfers between devices with their start and end apart: 12 -> 15, of which waited for: 5 -> 5; matrix products, arithmetic and copies ran while one was open for 2% -> 6% of each run, Pallas kernels for 9% -> 8%
where the time goes in v2:
time: 195 us; the launch traced here: 194 us
  starting transfers between devices  95.9 us (49%)
  blocking collectives  33.4 us (17%)
  waiting for transfers between devices  22.2 us (11%)
  local copies, waits for them, and re-layouts  19.8 us (10%)
  Pallas kernels  19.6 us (10%)
    ppermute x11, starting transfers between devices, moved(): return lax.ppermute(shard, axis, pairs)  48.4 us
    all_to_all x1, starting transfers between devices, on_device(): last = lax.all_to_all(column, ('zl', 'x', 'core'), 0, 0, tiled=True)  27.9 us
    all_gather x1, blocking collectives, on_device(): pats = lax.all_gather(pat, 'sec', axis=0)  19.7 us
    unnamed x1, blocking collectives  13.6 us
    unnamed x47, local copies, waits for them, and re-layouts  13.4 us
    all_to_all x1, waiting for transfers between devices, on_device(): last = lax.all_to_all(column, ('zl', 'x', 'core'), 0, 0, tiled=True)  11.9 us
    ppermute x11, waiting for transfers between devices, moved(): return lax.ppermute(shard, axis, pairs)  10.3 us
    all_to_all x1, starting transfers between devices, on_device(): lax.all_to_all(jnp.broadcast_to(qkv_weight.transpose(1, 0, 2), (8, 3, 24,...  6.85 us
  transfers between devices with their start and end apart: 15, of which 5 were waited for; matrix products, arithmetic and copies ran while one was open for 6% of the time, Pallas kernels for 8%

profile of v2, /device:TPU:1, one launch (start us, length us, event | category | flops | bytes accessed | tf_op | source)
XLA Modules:
  0.0 193.7 jit_solution(17098362143142038951)
XLA Ops:
  1.4 9.6 %collective-permute-start = (bf16[3,1,1,256]{3,2,1,0:T(2,128)(2,1)S(1)}, bf16[3,1,1,256]{3,2,1,0:T(2,128)(2,1)S(1)}, u32[]{:S(2)}, u32[]{:S(2)}) collective-permute-start(bf16[3,1,1,256]{3,2,1,0:T(2,128)(2,1)S(1)} %get-tuple-element.41), channel_id=1, source_target_pairs={{0,128},{128,256},{256,384},{1,129},{129,257},{257,385},{2,130},{1... | collective-permute-start | bytes 4616 | tf_op jit(solution)/shard_map/ppermute | solution.py:223
  14.1 6.9 %all-to-all-start = ((bf16[8,3,24,384]{3,2,1,0:T(8,128)(2,1)}), bf16[8,3,24,384]{3,2,1,0:T(8,128)(2,1)S(1)}, u32[]{:S(2)}, u32[]{:S(2)}) async-start(bf16[8,3,24,384]{3,2,1,0:T(8,128)(2,1)} %broadcast_in_dim.16), calls=%async_computation | async-start | bytes 884736 | tf_op jit(solution)/shard_map/all_to_all | solution.py:242
  26.1 3.1 %collective-permute-start.3 = (bf16[3,1,130,256]{3,2,1,0:T(8,128)(2,1)S(1)}, bf16[3,1,130,256]{3,2,1,0:T(8,128)(2,1)S(1)}, u32[]{:S(2)}, u32[]{:S(2)}) collective-permute-start(bf16[3,1,130,256]{3,2,1,0:T(8,128)(2,1)S(1)} %pad_maximum_fusion.v0), channel_id=1, source_target_pairs={{0,1},{1,2},{2,3},{3,4},{4,5},{5,6},{6,7},{7,8},{8,9},{9,10},{10,1... | collective-permute-start | bytes 599048 | tf_op jit(solution)/shard_map/ppermute | solution.py:223
  29.2 3.2 %collective-permute-start.2 = (bf16[3,1,130,256]{3,2,1,0:T(8,128)(2,1)S(1)}, bf16[3,1,130,256]{3,2,1,0:T(8,128)(2,1)S(1)}, u32[]{:S(2)}, u32[]{:S(2)}) collective-permute-start(bf16[3,1,130,256]{3,2,1,0:T(8,128)(2,1)S(1)} %pad_maximum_fusion.v0), channel_id=1, source_target_pairs={{0,2},{1,3},{2,4},{3,5},{4,6},{5,7},{6,8},{7,9},{8,10},{9,11},{10,... | collective-permute-start | bytes 599048 | tf_op jit(solution)/shard_map/ppermute | solution.py:223
  34.3 9.4 %collective-permute-start.5 = (bf16[1536,128]{1,0:T(8,128)(2,1)}, bf16[1536,128]{1,0:T(8,128)(2,1)S(1)}, u32[]{:S(2)}, u32[]{:S(2)}) collective-permute-start(bf16[1536,128]{1,0:T(8,128)(2,1)} %shard_map.116.c0), channel_id=1, source_target_pairs={{0,384},{128,0},{256,128},{384,256},{1,385},{129,1},{257,129},{385... | collective-permute-start | bytes 1179656 | tf_op jit(solution)/shard_map/ppermute | solution.py:223
  49.0 13.6 %all-reduce.3 = s32[16]{0:T(128)S(1)} all-reduce(s32[16]{0:T(128)S(1)} %dynamic-update-slice), channel_id=1, replica_groups=mesh['sec'=4,'zl'=4,'x'=4,'y'=4,'core'=2] {'x','y'}, use_global_device_ids=true, to_apply=%add.3 | all-reduce | flops 16 | bytes 128
  64.5 6.4 %shard_map.112 = (bf16[256,32]{1,0:T(8,128)(2,1)S(1)}, bf16[64,128]{1,0:T(8,128)(2,1)S(1)}) custom-call(f32[1]{0:T(128)S(6)} %div.9.level, bf16[3,1,130,256]{3,2,1,0:T(8,128)(2,1)S(1)} %copy-done.4, bf16[3,1,130,256]{3,2,1,0:T(8,128)(2,1)S(1)} %copy-done.2, bf16[3,1,130,256]{3,2,1,0:T(8,128)(2,1)S(1)} %pad_maximum_fusion.v0, ...), custom_call_target="tpu_custom_call" | custom-call | flops 10000000000 | bytes 1000000 | tf_op jit(solution)/shard_map/pallas_call | solution.py:279
  71.7 2.0 %shard_map.114 = (bf16[1024,192]{1,0:T(8,128)(2,1)S(1)}, bf16[1024,192]{1,0:T(8,128)(2,1)S(1)}, f32[64,64]{1,0:T(8,128)S(1)}) custom-call(s32[1]{0:T(128)} %bitcast.9.place, bf16[64,3072]{1,0:T(8,128)(2,1)S(1)} %copy-done.9, bf16[256,3072]{1,0:T(8,128)(2,1)S(1)} %copy-done.8, f32[16,256]{1,0:T(8,128)S(1)} %pad_maximum_fusion.1.temb), custom_call_target="tpu_custom_call" | custom-call | flops 1000000000 | bytes 3000000 | tf_op jit(solution)/shard_map/pallas_call | solution.py:256
  73.8 3.2 %shard_map.115 = bf16[1024,1152]{1,0:T(8,128)(2,1)} custom-call(bf16[1024,192]{1,0:T(8,128)(2,1)S(1)} %get-tuple-element.24.a_hi, bf16[1024,192]{1,0:T(8,128)(2,1)S(1)} %get-tuple-element.25.a_lo, bf16[3,192,384]{2,1,0:T(8,128)(2,1)S(1)} %bitcast.36), custom_call_target="tpu_custom_call" | custom-call | flops 1000000000 | bytes 5000000 | tf_op jit(solution)/shard_map/pallas_call | solution.py:268
  77.0 6.1 %all-to-all-start.1 = ((bf16[16,64,1152]{2,1,0:T(8,128)(2,1)}), bf16[16,64,1152]{2,1,0:T(8,128)(2,1)S(1)}, u32[]{:S(2)}, u32[]{:S(2)}) async-start(bf16[16,64,1152]{2,1,0:T(8,128)(2,1)} %bitcast.17), calls=%async_computation.1 | async-start | bytes 4718592 | tf_op jit(solution)/shard_map/all_to_all | solution.py:296
  83.1 19.7 %all-gather = bf16[256,128]{1,0:T(8,128)(2,1)} all-gather(bf16[64,128]{1,0:T(8,128)(2,1)S(1)} %get-tuple-element.26), channel_id=2, replica_groups=mesh['sec'=4,'zl'=4,'x'=4,'y'=4,'core'=2] {'sec'}, dimensions={0}, use_global_device_ids=true | all-gather | bytes 81920 | tf_op jit(solution)/shard_map/all_gather | solution.py:297
  102.9 4.7 %collective-permute-start.7 = (bf16[768,128]{1,0:T(8,128)(2,1)S(1)}, bf16[768,128]{1,0:T(8,128)(2,1)S(1)}, u32[]{:S(2)}, u32[]{:S(2)}) collective-permute-start(bf16[768,128]{1,0:T(8,128)(2,1)S(1)} %slice.15), channel_id=1, source_target_pairs={{0,384},{128,0},{256,128},{384,256},{1,385},{129,1},{257,129},{385... | collective-permute-start | bytes 589832 | tf_op jit(solution)/shard_map/ppermute | solution.py:223
  107.6 4.7 %collective-permute-start.6 = (bf16[768,128]{1,0:T(8,128)(2,1)S(1)}, bf16[768,128]{1,0:T(8,128)(2,1)S(1)}, u32[]{:S(2)}, u32[]{:S(2)}) collective-permute-start(bf16[768,128]{1,0:T(8,128)(2,1)S(1)} %slice.14), channel_id=1, source_target_pairs={{0,128},{128,256},{256,384},{384,0},{1,129},{129,257},{257,385},{3... | collective-permute-start | bytes 589832 | tf_op jit(solution)/shard_map/ppermute | solution.py:223
  112.3 2.9 %collective-permute-done.7.far_b = bf16[768,128]{1,0:T(8,128)(2,1)S(1)} collective-permute-done((bf16[768,128]{1,0:T(8,128)(2,1)S(1)}, bf16[768,128]{1,0:T(8,128)(2,1)S(1)}, u32[]{:S(2)}, u32[]{:S(2)}) %collective-permute-start.7) | collective-permute-done | bytes 196640 | tf_op jit(solution)/shard_map/ppermute | solution.py:223
  115.8 2.6 %collective-permute-done.6.far_a = bf16[768,128]{1,0:T(8,128)(2,1)S(1)} collective-permute-done((bf16[768,128]{1,0:T(8,128)(2,1)S(1)}, bf16[768,128]{1,0:T(8,128)(2,1)S(1)}, u32[]{:S(2)}, u32[]{:S(2)}) %collective-permute-start.6) | collective-permute-done | bytes 196640 | tf_op jit(solution)/shard_map/ppermute | solution.py:223
  120.7 3.4 %shard_map.117.att = bf16[512,384]{1,0:T(8,128)(2,1)} custom-call(bf16[4,64,128]{2,1,0:T(8,128)(2,1)S(1)} %bitcast.37, bf16[16,64,1152]{2,1,0:T(8,128)(2,1)S(1)} %all-to-all-done.1.parts, f32[64,64]{1,0:T(8,128)S(1)} %copy-done.16), custom_call_target="tpu_custom_call" | custom-call | flops 4000000000 | bytes 1000000 | tf_op jit(solution)/shard_map/pallas_call | solution.py:302
  124.2 6.7 %all-to-all-start.2 = ((bf16[4,128,384]{2,1,0:T(8,128)(2,1)}), bf16[4,128,384]{2,1,0:T(8,128)(2,1)S(1)}, u32[]{:S(2)}, u32[]{:S(2)}) async-start(bf16[4,128,384]{2,1,0:T(8,128)(2,1)} %bitcast.18), calls=%async_computation.2 | async-start | bytes 786432 | tf_op jit(solution)/shard_map/all_to_all | solution.py:305
  132.8 2.3 %shard_map.118 = (bf16[384,384]{1,0:T(8,128)(2,1)S(1)}, bf16[384,384]{1,0:T(8,128)(2,1)S(1)}, bf16[384,384]{1,0:T(8,128)(2,1)S(1)}, bf16[384,384]{1,0:T(8,128)(2,1)S(1)}) custom-call(s32[2]{0:T(128)S(1)} %pad_add_fusion.place, bf16[512,384]{1,0:T(8,128)(2,1)} %shard_map.117.att, bf16[1536,128]{1,0:T(8,128)(2,1)S(1)} %copy-done, ...), custom_call_target="tpu_custom_call" | custom-call | flops 1000000000 | bytes 5000000 | tf_op jit(solution)/shard_map/pallas_call | solution.py:307
  135.1 3.1 %collective-permute-start.8 = (bf16[384,384]{1,0:T(8,128)(2,1)S(1)}, bf16[384,384]{1,0:T(8,128)(2,1)S(1)}, u32[]{:S(2)}, u32[]{:S(2)}) collective-permute-start(bf16[384,384]{1,0:T(8,128)(2,1)S(1)} %get-tuple-element.38), channel_id=1, source_target_pairs={{0,2},{2,4},{4,6},{6,0},{1,3},{3,5},{5,7},{7,1},{8,10},{10,12},{12... | collective-permute-start | bytes 884744 | tf_op jit(solution)/shard_map/ppermute | solution.py:223
  138.2 4.7 %collective-permute-start.9 = (bf16[384,384]{1,0:T(8,128)(2,1)S(1)}, bf16[384,384]{1,0:T(8,128)(2,1)S(1)}, u32[]{:S(2)}, u32[]{:S(2)}) collective-permute-start(bf16[384,384]{1,0:T(8,128)(2,1)S(1)} %get-tuple-element.39), channel_id=1, source_target_pairs={{0,4},{2,6},{4,0},{6,2},{1,5},{3,7},{5,1},{7,3},{8,12},{10,14},{12... | collective-permute-start | bytes 884744 | tf_op jit(solution)/shard_map/ppermute | solution.py:223
  142.9 2.7 %collective-permute-start.10 = (bf16[384,384]{1,0:T(8,128)(2,1)S(1)}, bf16[384,384]{1,0:T(8,128)(2,1)S(1)}, u32[]{:S(2)}, u32[]{:S(2)}) collective-permute-start(bf16[384,384]{1,0:T(8,128)(2,1)S(1)} %get-tuple-element.40), channel_id=1, source_target_pairs={{0,6},{2,0},{4,2},{6,4},{1,7},{3,1},{5,3},{7,5},{8,14},{10,8},{12,... | collective-permute-start | bytes 884744 | tf_op jit(solution)/shard_map/ppermute | solution.py:223
  145.6 2.9 %collective-permute-done.9 = bf16[384,384]{1,0:T(8,128)(2,1)S(1)} collective-permute-done((bf16[384,384]{1,0:T(8,128)(2,1)S(1)}, bf16[384,384]{1,0:T(8,128)(2,1)S(1)}, u32[]{:S(2)}, u32[]{:S(2)}) %collective-permute-start.9) | collective-permute-done | bytes 294944 | tf_op jit(solution)/shard_map/ppermute | solution.py:223
  151.4 27.9 %all-to-all-start.3 = ((bf16[32,12,384]{2,1,0:T(8,128)(2,1)}), bf16[32,12,384]{2,1,0:T(8,128)(2,1)S(1)}, u32[]{:S(2)}, u32[]{:S(2)}) async-start(bf16[32,12,384]{2,1,0:T(8,128)(2,1)} %reshape.55), calls=%async_computation.3 | async-start | bytes 786432 | tf_op jit(solution)/shard_map/all_to_all | solution.py:326
  181.1 11.9 %all-to-all-done.3 = bf16[32,12,384]{2,1,0:T(8,128)(2,1)S(1)} async-done(((bf16[32,12,384]{2,1,0:T(8,128)(2,1)}), bf16[32,12,384]{2,1,0:T(8,128)(2,1)S(1)}, u32[]{:S(2)}, u32[]{:S(2)}) %all-to-all-start.3) | async-done | bytes 294944 | tf_op jit(solution)/shard_map/all_to_all | solution.py:326
  (87 shorter events, 28.3 us)
Async XLA Ops:
  0.6 25.4 %copy-start.18 = (bf16[3,1,128,256]{3,2,1,0:T(8,128)(2,1)S(1)}, bf16[3,1,128,256]{3,2,1,0:T(8,128)(2,1)}, u32[]{:S(2)}) copy-start(bf16[3,1,128,256]{3,2,1,0:T(8,128)(2,1)} %param.9) | copy-start | bytes 589828
  0.6 23.1 %copy-start.17 = (bf16[1,128,1536]{2,1,0:T(8,128)(2,1)S(1)}, bf16[1,128,1536]{2,1,0:T(8,128)(2,1)}, u32[]{:S(2)}) copy-start(bf16[1,128,1536]{2,1,0:T(8,128)(2,1)} %param.17) | copy-start | bytes 1179652
  1.4 24.6 %collective-permute-start = (bf16[3,1,1,256]{3,2,1,0:T(2,128)(2,1)S(1)}, bf16[3,1,1,256]{3,2,1,0:T(2,128)(2,1)S(1)}, u32[]{:S(2)}, u32[]{:S(2)}) collective-permute-start(bf16[3,1,1,256]{3,2,1,0:T(2,128)(2,1)S(1)} %get-tuple-element.41), channel_id=1, source_target_pairs={{0,128},{128,256},{256,384},{1,129},{129,257},{257,385},{2,130},{1... | collective-permute-start | bytes 4616 | tf_op jit(solution)/shard_map/ppermute | solution.py:223
  11.1 15.0 %collective-permute-start.1 = (bf16[3,1,1,256]{3,2,1,0:T(2,128)(2,1)S(1)}, bf16[3,1,1,256]{3,2,1,0:T(2,128)(2,1)S(1)}, u32[]{:S(2)}, u32[]{:S(2)}) collective-permute-start(bf16[3,1,1,256]{3,2,1,0:T(2,128)(2,1)S(1)} %get-tuple-element.42), channel_id=1, source_target_pairs={{128,0},{256,128},{384,256},{129,1},{257,129},{385,257},{130,2},{2... | collective-permute-start | bytes 4616 | tf_op jit(solution)/shard_map/ppermute | solution.py:223
  12.4 50.3 %copy-start.10 = (bf16[128,8,8,16]{0,3,2,1:T(8,128)(2,1)S(1)}, bf16[128,8,8,16]{0,3,2,1:T(8,128)(2,1)}, u32[]{:S(2)}) copy-start(bf16[128,8,8,16]{0,3,2,1:T(8,128)(2,1)} %param.11) | copy-start | bytes 786436
  14.1 59.7 %all-to-all-start = ((bf16[8,3,24,384]{3,2,1,0:T(8,128)(2,1)}), bf16[8,3,24,384]{3,2,1,0:T(8,128)(2,1)S(1)}, u32[]{:S(2)}, u32[]{:S(2)}) async-start(bf16[8,3,24,384]{3,2,1,0:T(8,128)(2,1)} %broadcast_in_dim.16), calls=%async_computation | async-start | bytes 884736 | tf_op jit(solution)/shard_map/all_to_all | solution.py:242
  26.1 6.5 %copy-start.19 = (bf16[3,1,1,256]{3,2,1,0:T(2,128)(2,1)}, bf16[3,1,1,256]{3,2,1,0:T(2,128)(2,1)S(1)}, u32[]{:S(2)}) copy-start(bf16[3,1,1,256]{3,2,1,0:T(2,128)(2,1)S(1)} %collective-permute-done.rest_0_) | copy-start | bytes 4612
  26.1 6.5 %copy-start.20 = (bf16[3,1,1,256]{3,2,1,0:T(2,128)(2,1)}, bf16[3,1,1,256]{3,2,1,0:T(2,128)(2,1)S(1)}, u32[]{:S(2)}) copy-start(bf16[3,1,1,256]{3,2,1,0:T(2,128)(2,1)S(1)} %collective-permute-done.1.rest_1_) | copy-start | bytes 4612
  26.1 17.6 %collective-permute-start.3 = (bf16[3,1,130,256]{3,2,1,0:T(8,128)(2,1)S(1)}, bf16[3,1,130,256]{3,2,1,0:T(8,128)(2,1)S(1)}, u32[]{:S(2)}, u32[]{:S(2)}) collective-permute-start(bf16[3,1,130,256]{3,2,1,0:T(8,128)(2,1)S(1)} %pad_maximum_fusion.v0), channel_id=1, source_target_pairs={{0,1},{1,2},{2,3},{3,4},{4,5},{5,6},{6,7},{7,8},{8,9},{9,10},{10,1... | collective-permute-start | bytes 599048 | tf_op jit(solution)/shard_map/ppermute | solution.py:223
  29.2 14.5 %collective-permute-start.2 = (bf16[3,1,130,256]{3,2,1,0:T(8,128)(2,1)S(1)}, bf16[3,1,130,256]{3,2,1,0:T(8,128)(2,1)S(1)}, u32[]{:S(2)}, u32[]{:S(2)}) collective-permute-start(bf16[3,1,130,256]{3,2,1,0:T(8,128)(2,1)S(1)} %pad_maximum_fusion.v0), channel_id=1, source_target_pairs={{0,2},{1,3},{2,4},{3,5},{4,6},{5,7},{6,8},{7,9},{8,10},{9,11},{10,... | collective-permute-start | bytes 599048 | tf_op jit(solution)/shard_map/ppermute | solution.py:223
  34.3 42.7 %collective-permute-start.5 = (bf16[1536,128]{1,0:T(8,128)(2,1)}, bf16[1536,128]{1,0:T(8,128)(2,1)S(1)}, u32[]{:S(2)}, u32[]{:S(2)}) collective-permute-start(bf16[1536,128]{1,0:T(8,128)(2,1)} %shard_map.116.c0), channel_id=1, source_target_pairs={{0,384},{128,0},{256,128},{384,256},{1,385},{129,1},{257,129},{385... | collective-permute-start | bytes 1179656 | tf_op jit(solution)/shard_map/ppermute | solution.py:223
  47.1 29.9 %collective-permute-start.4 = (bf16[1536,128]{1,0:T(8,128)(2,1)}, bf16[1536,128]{1,0:T(8,128)(2,1)S(1)}, u32[]{:S(2)}, u32[]{:S(2)}) collective-permute-start(bf16[1536,128]{1,0:T(8,128)(2,1)} %shard_map.116.c0), channel_id=1, source_target_pairs={{0,128},{128,256},{256,384},{384,0},{1,129},{129,257},{257,385},{3... | collective-permute-start | bytes 1179656 | tf_op jit(solution)/shard_map/ppermute | solution.py:223
  64.5 7.2 %copy-start.8 = (bf16[256,3072]{1,0:T(8,128)(2,1)S(1)}, bf16[256,3072]{1,0:T(8,128)(2,1)}, u32[]{:S(2)}) copy-start(bf16[256,3072]{1,0:T(8,128)(2,1)} %mod.1) | copy-start | bytes 4718596
  64.5 7.2 %copy-start.9 = (bf16[64,3072]{1,0:T(8,128)(2,1)S(1)}, bf16[64,3072]{1,0:T(8,128)(2,1)}, u32[]{:S(2)}) copy-start(bf16[64,3072]{1,0:T(8,128)(2,1)} %embed.1) | copy-start | bytes 1179652
  77.0 42.1 %all-to-all-start.1 = ((bf16[16,64,1152]{2,1,0:T(8,128)(2,1)}), bf16[16,64,1152]{2,1,0:T(8,128)(2,1)S(1)}, u32[]{:S(2)}, u32[]{:S(2)}) async-start(bf16[16,64,1152]{2,1,0:T(8,128)(2,1)} %bitcast.17), calls=%async_computation.1 | async-start | bytes 4718592 | tf_op jit(solution)/shard_map/all_to_all | solution.py:296
  102.9 12.3 %collective-permute-start.7 = (bf16[768,128]{1,0:T(8,128)(2,1)S(1)}, bf16[768,128]{1,0:T(8,128)(2,1)S(1)}, u32[]{:S(2)}, u32[]{:S(2)}) collective-permute-start(bf16[768,128]{1,0:T(8,128)(2,1)S(1)} %slice.15), channel_id=1, source_target_pairs={{0,384},{128,0},{256,128},{384,256},{1,385},{129,1},{257,129},{385... | collective-permute-start | bytes 589832 | tf_op jit(solution)/shard_map/ppermute | solution.py:223
  107.6 10.8 %collective-permute-start.6 = (bf16[768,128]{1,0:T(8,128)(2,1)S(1)}, bf16[768,128]{1,0:T(8,128)(2,1)S(1)}, u32[]{:S(2)}, u32[]{:S(2)}) collective-permute-start(bf16[768,128]{1,0:T(8,128)(2,1)S(1)} %slice.14), channel_id=1, source_target_pairs={{0,128},{128,256},{256,384},{384,0},{1,129},{129,257},{257,385},{3... | collective-permute-start | bytes 589832 | tf_op jit(solution)/shard_map/ppermute | solution.py:223
  120.7 10.2 %copy-start = (bf16[1536,128]{1,0:T(8,128)(2,1)S(1)}, bf16[1536,128]{1,0:T(8,128)(2,1)}, u32[]{:S(2)}) copy-start(bf16[1536,128]{1,0:T(8,128)(2,1)} %shard_map.116.c0) | copy-start | bytes 1179652
  124.2 27.2 %all-to-all-start.2 = ((bf16[4,128,384]{2,1,0:T(8,128)(2,1)}), bf16[4,128,384]{2,1,0:T(8,128)(2,1)S(1)}, u32[]{:S(2)}, u32[]{:S(2)}) async-start(bf16[4,128,384]{2,1,0:T(8,128)(2,1)} %bitcast.18), calls=%async_computation.2 | async-start | bytes 786432 | tf_op jit(solution)/shard_map/all_to_all | solution.py:305
  135.1 44.1 %copy-start.7 = (bf16[256,32]{1,0:T(8,128)(2,1)S(1)}, bf16[256,32]{1,0:T(8,128)(2,1)}, u32[]{:S(2)}) copy-start(bf16[256,32]{1,0:T(8,128)(2,1)} %copy-done.6) | copy-start | bytes 49156
  135.1 10.5 %collective-permute-start.8 = (bf16[384,384]{1,0:T(8,128)(2,1)S(1)}, bf16[384,384]{1,0:T(8,128)(2,1)S(1)}, u32[]{:S(2)}, u32[]{:S(2)}) collective-permute-start(bf16[384,384]{1,0:T(8,128)(2,1)S(1)} %get-tuple-element.38), channel_id=1, source_target_pairs={{0,2},{2,4},{4,6},{6,0},{1,3},{3,5},{5,7},{7,1},{8,10},{10,12},{12... | collective-permute-start | bytes 884744 | tf_op jit(solution)/shard_map/ppermute | solution.py:223
  138.2 10.4 %collective-permute-start.9 = (bf16[384,384]{1,0:T(8,128)(2,1)S(1)}, bf16[384,384]{1,0:T(8,128)(2,1)S(1)}, u32[]{:S(2)}, u32[]{:S(2)}) collective-permute-start(bf16[384,384]{1,0:T(8,128)(2,1)S(1)} %get-tuple-element.39), channel_id=1, source_target_pairs={{0,4},{2,6},{4,0},{6,2},{1,5},{3,7},{5,1},{7,3},{8,12},{10,14},{12... | collective-permute-start | bytes 884744 | tf_op jit(solution)/shard_map/ppermute | solution.py:223
  142.9 7.5 %collective-permute-start.10 = (bf16[384,384]{1,0:T(8,128)(2,1)S(1)}, bf16[384,384]{1,0:T(8,128)(2,1)S(1)}, u32[]{:S(2)}, u32[]{:S(2)}) collective-permute-start(bf16[384,384]{1,0:T(8,128)(2,1)S(1)} %get-tuple-element.40), channel_id=1, source_target_pairs={{0,6},{2,0},{4,2},{6,4},{1,7},{3,1},{5,3},{7,5},{8,14},{10,8},{12,... | collective-permute-start | bytes 884744 | tf_op jit(solution)/shard_map/ppermute | solution.py:223
  151.4 41.6 %all-to-all-start.3 = ((bf16[32,12,384]{2,1,0:T(8,128)(2,1)}), bf16[32,12,384]{2,1,0:T(8,128)(2,1)S(1)}, u32[]{:S(2)}, u32[]{:S(2)}) async-start(bf16[32,12,384]{2,1,0:T(8,128)(2,1)} %reshape.55), calls=%async_computation.3 | async-start | bytes 786432 | tf_op jit(solution)/shard_map/all_to_all | solution.py:326
  (12 other events, 12.0 us)

commit v3 on v2

--- a/solution.py
+++ b/solution.py
@@ -26,7 +26,7 @@
         out_specs=[VMEM] * len(out_shape) if several else VMEM,
         scratch_shapes=list(scratch),
         compiler_params=pltpu.CompilerParams(vmem_limit_bytes=VMEM_BYTES),
-        cost_estimate=pl.CostEstimate(flops=flops, bytes_accessed=nbytes, transcendentals=0),
+        cost_estimate=pl.CostEstimate(flops=flops // 10**6, bytes_accessed=nbytes // 10**5, transcendentals=0),
     )
 
 
@@ -181,8 +181,8 @@
         att[:, 128 * h : 128 * h + 128] = out.astype(BF16)
 
 
-def grad_body(place, att, c0, c_up, c_down, far_a, far_b, out0, out1, out2, out3, full):
-    sec, y = place[0], place[1]
+def grad_body(place, att, c0, c_up, c_down, far_a, far_b, out, full, blocks):
+    sec, y, core = place[0], place[1], place[2]
     sides = []
     for step in (0, 3, 1, 2):
         row = pl.multiple_of(((sec + step) & 3) * 128, 128)
@@ -192,26 +192,21 @@
         rows = slice(768 * half, 768 * half + 768)
         lhs = jnp.concatenate([c0[rows], c_up[rows], c_down[rows], far[...]], axis=1)
         full[rows] = jnp.dot(lhs, rhs, preferred_element_type=F32)
-    for by, out in enumerate((out0, out1, out2, out3)):
-        to_y = (y + by) & 3
-        for zx in range(0, 16, 2):
-            pair = [
-                full[pl.ds(pl.multiple_of(24 * to_y + 96 * k, 8), 24), :] for k in (zx, zx + 1)
-            ]
-            out[24 * zx : 24 * zx + 48] = jnp.concatenate(pair, axis=0).astype(BF16)
-
-
-def gate_body(value, *rest):
-    rest[-1][...] = value[...]
-
-
-def gated(value, *deps):
-    return pl.pallas_call(
-        gate_body,
-        out_shape=jax.ShapeDtypeStruct(value.shape, value.dtype),
-        in_specs=[VMEM] + [ANY] * len(deps),
-        out_specs=VMEM,
-    )(value, *deps)
+    for to_core in range(2):
+        for to_y in range(4):
+            slot = ((to_core + core) & 1) * 4 + ((to_y - y) & 3)
+            for zx in range(16):
+                first = 12 * (8 * zx + 2 * to_y + to_core)
+                blocks[slot, 12 * zx : 12 * zx + 12] = full[first : first + 12]
+    for slot in range(8):
+        out[slot] = blocks[slot].astype(BF16)
+
+
+def pack_body(cot, bottom, top, up, down):
+    up[0:1536] = cot[...]
+    down[0:1536] = cot[...]
+    up[1536:1552] = bottom[...]
+    down[1536:1552] = top[...]
 
 
 def together(*values):
@@ -234,20 +229,20 @@
     qkv_weight,
     cotangent,
 ):
-    above = moved(video[:, :, 127:128], ("sec",), 4, 1, False)
-    below = moved(video[:, :, 0:1], ("sec",), 4, -1, False)
-    v0 = jnp.concatenate([video, above, below], axis=2)
-    v1, v2 = moved(v0, SEQ, 128, 1, False), moved(v0, SEQ, 128, 2, False)
+    rims = [
+        jnp.pad(video[:, 0, row].reshape(6, 128), ((0, 10), (0, 0))) for row in (127, 0)
+    ]
+    cot, cot_top = call(
+        pack_body, [jax.ShapeDtypeStruct((1552, 128), BF16)] * 2, 0, 3, 0, 10**6
+    )(cotangent[0].T, *rims)
+    c_up = moved(cot, "sec", 4, 1, True)
+    c_down = moved(cot_top, "sec", 4, -1, True)
 
     rows = lax.all_to_all(
         jnp.broadcast_to(qkv_weight.transpose(1, 0, 2), (8, 3, 24, 384)), ("zl", "core"), 0, 0, tiled=True
     )
     rows = rows.transpose(1, 0, 2, 3).reshape(3, 192, 384)
-    stamps = lax.all_gather(gated(timesteps, v1, v2), ("x", "y"), axis=0, tiled=True)
-
-    cot = gated(cotangent[0].T, above, below)
-    c_up = moved(cot, "sec", 4, 1, True)
-    c_down = moved(cot, "sec", 4, -1, True)
+    stamps = lax.all_gather(timesteps, ("x", "y"), axis=0, tiled=True)
 
     frequency = jnp.exp(-math.log(10000.0) * jnp.arange(128, dtype=F32) / 128)
     angles = stamps.astype(F32)[:, None] * frequency[None, :]
@@ -268,6 +263,14 @@
     partial = call(
         fold_body, jax.ShapeDtypeStruct((1024, 1152), BF16), 0, 3, 10**9, 5 * 10**6
     )(a_hi, a_lo, rows)
+    partial, c_up, c_down = together(partial, c_up, c_down)
+    sec = lax.axis_index("sec").astype(jnp.int32)[None]
+    above = jnp.where(sec[0] == 0, 0, c_up[1536:1542]).astype(BF16).reshape(3, 1, 1, 256)
+    below = jnp.where(sec[0] == 3, 0, c_down[1536:1542]).astype(BF16).reshape(3, 1, 1, 256)
+    v0 = jnp.concatenate([video, above, below], axis=2)
+    v1, v2 = moved(v0, SEQ, 128, 1, False), moved(v0, SEQ, 128, 2, False)
+    partial, v1, v2 = together(partial, v1, v2)
+
     taps = conv_weight.reshape(128, 3, 3, 3, 3).transpose(0, 3, 4, 1, 2).reshape(128, 3, 27)
     taps = jnp.pad(taps, ((0, 0), (0, 0), (0, 5))).reshape(128, 96)
     conv = jnp.concatenate(
@@ -292,28 +295,26 @@
     )(level, v2, v1, v0, conv, down, noise_t)
     latents = lat.reshape(16, 16, 32).transpose(1, 0, 2)[:, None]
 
-    pat, partial, c_up, c_down = together(pat, partial, c_up, c_down)
+    far_a = moved(c_up[0:768], "sec", 4, 1, True)
+    far_b = moved(c_down[768:1536], "sec", 4, -1, True)
+    pat, far_a, far_b = together(pat, far_a, far_b)
     parts = lax.all_to_all(partial.reshape(16, 64, 1152), ("x", "y"), 0, 0, tiled=True)
     pats = lax.all_gather(pat, "sec", axis=0)
-    pats, c_up, c_down = together(pats, c_up, c_down)
-    far_a = moved(c_up[0:768], "sec", 4, 1, True)
-    far_b = moved(c_down[768:1536], "sec", 4, -1, True)
-    parts, far_a, far_b = together(parts, far_a, far_b)
     att = call(
         attend_body, jax.ShapeDtypeStruct((512, 384), BF16), 0, 3, 4 * 10**9, 10**6
     )(pats, parts, gram)
     attended = lax.all_to_all(att, "sec", split_axis=0, concat_axis=1, tiled=True)
 
-    sums = call(
+    blocks = call(
         grad_body,
-        [jax.ShapeDtypeStruct((384, 384), BF16)] * 4,
+        jax.ShapeDtypeStruct((8, 192, 384), BF16),
         1,
         6,
         10**9,
         5 * 10**6,
-        [pltpu.VMEM((1536, 384), F32)],
+        [pltpu.VMEM((1536, 384), F32), pltpu.VMEM((8, 192, 384), F32)],
     )(
-        jnp.stack([lax.axis_index("sec"), lax.axis_index("y")]).astype(jnp.int32),
+        jnp.stack([sec[0], lax.axis_index("y"), lax.axis_index("core")]).astype(jnp.int32),
         att,
         cot,
         c_up,
@@ -321,9 +322,11 @@
         far_a,
         far_b,
     )
-    got = [moved(sums[by], "y", 4, by, True).astype(F32) for by in range(1, 4)]
-    column = sum(got, sums[0].astype(F32)).astype(BF16).reshape(32, 12, 384)
-    last = lax.all_to_all(column, ("zl", "x", "core"), 0, 0, tiled=True)
+    other = moved(blocks[4:8], "core", 2, 1, True)
+    pair_sum = (blocks[0:4].astype(F32) + other.astype(F32)).astype(BF16)
+    got = [moved(pair_sum[by], "y", 4, by, True) for by in range(1, 4)]
+    row_sum = sum([g.astype(F32) for g in got], pair_sum[0].astype(F32)).astype(BF16)
+    last = lax.all_to_all(row_sum.reshape(16, 12, 384), ("zl", "x"), 0, 0, tiled=True)
     out_grad = jnp.sum(last.astype(F32), axis=0)
     return (latents, attended[None], out_grad)
 

time: 195 us -> 184 us (0.944)
  starting transfers between devices: 95.9 us -> 85.8 us
    all_to_all x1, starting transfers between devices: 27.9 us -> 16.6 us  [on_device(): lax.all_to_all(row_sum.reshape(16, 12, 384), ('zl', 'x'), 0, 0, tiled=True)]
    ppermute x11 -> x10, starting transfers between devices: 48.4 us -> 38 us  [moved(): return lax.ppermute(shard, axis, pairs)]
    all_to_all x1, starting transfers between devices: 6.09 us -> 13.9 us  [on_device(): lax.all_to_all(partial.reshape(16, 64, 1152), ('x', 'y'), 0, 0, tiled=True)]
    all_to_all x1, waiting for transfers between devices: 0.01 us -> 6.69 us  [on_device(): lax.all_to_all(jnp.broadcast_to(qkv_weight.transpose(1, 0, 2), (8, 3, 24,...]
    all_to_all x1, waiting for transfers between devices: 11.9 us -> 6.45 us  [on_device(): lax.all_to_all(row_sum.reshape(16, 12, 384), ('zl', 'x'), 0, 0, tiled=True)]
    all_to_all x1, starting transfers between devices: 6.85 us -> 11 us  [on_device(): lax.all_to_all(jnp.broadcast_to(qkv_weight.transpose(1, 0, 2), (8, 3, 24,...]
    ppermute x11 -> x10, waiting for transfers between devices: 10.3 us -> 7.52 us  [moved(): return lax.ppermute(shard, axis, pairs)]
    unnamed x47 -> x51, local copies, waits for them, and re-layouts: 13.4 us -> 11.8 us
  transfers between devices with their start and end apart: 15 -> 14, of which waited for: 5 -> 6; matrix products, arithmetic and copies ran while one was open for 6% -> 6% of each run, Pallas kernels for 8% -> 7%
where the time goes in v3:
time: 184 us; the launch traced here: 182 us
  starting transfers between devices  85.8 us (47%)
  blocking collectives  32.7 us (18%)
  local copies, waits for them, and re-layouts  21.1 us (11%)
  waiting for transfers between devices  20.9 us (11%)
  Pallas kernels  18.5 us (10%)
    ppermute x10, starting transfers between devices, moved(): return lax.ppermute(shard, axis, pairs)  38 us
    all_gather x1, blocking collectives, on_device(): pats = lax.all_gather(pat, 'sec', axis=0)  19 us
    all_to_all x1, starting transfers between devices, on_device(): lax.all_to_all(row_sum.reshape(16, 12, 384), ('zl', 'x'), 0, 0, tiled=True)  16.6 us
    all_to_all x1, starting transfers between devices, on_device(): lax.all_to_all(partial.reshape(16, 64, 1152), ('x', 'y'), 0, 0, tiled=True)  13.9 us
    unnamed x1, blocking collectives  13.7 us
    unnamed x51, local copies, waits for them, and re-layouts  11.8 us
    all_to_all x1, starting transfers between devices, on_device(): lax.all_to_all(jnp.broadcast_to(qkv_weight.transpose(1, 0, 2), (8, 3, 24,...  11 us
    ppermute x10, waiting for transfers between devices, moved(): return lax.ppermute(shard, axis, pairs)  7.52 us
  transfers between devices with their start and end apart: 14, of which 6 were waited for; matrix products, arithmetic and copies ran while one was open for 6% of the time, Pallas kernels for 7%

profile of v3, /device:TPU:1, one launch (start us, length us, event | category | flops | bytes accessed | tf_op | source)
XLA Modules:
  0.0 181.8 jit_solution(9367276053884449930)
XLA Ops:
  2.3 11.0 %all-to-all-start = ((bf16[8,3,24,384]{3,2,1,0:T(8,128)(2,1)}), bf16[8,3,24,384]{3,2,1,0:T(8,128)(2,1)}, u32[]{:S(2)}, u32[]{:S(2)}) async-start(bf16[8,3,24,384]{3,2,1,0:T(8,128)(2,1)} %broadcast_in_dim.23), calls=%async_computation | async-start | bytes 884736 | tf_op jit(solution)/shard_map/all_to_all | solution.py:241
  15.2 7.1 %collective-permute-start.1 = (bf16[1552,128]{1,0:T(8,128)(2,1)}, bf16[1552,128]{1,0:T(8,128)(2,1)S(1)}, u32[]{:S(2)}, u32[]{:S(2)}) collective-permute-start(bf16[1552,128]{1,0:T(8,128)(2,1)} %get-tuple-element.22), channel_id=1, source_target_pairs={{0,384},{128,0},{256,128},{384,256},{1,385},{129,1},{257,129},{385... | collective-permute-start | bytes 1191944 | tf_op jit(solution)/shard_map/ppermute | solution.py:218
  25.0 2.1 %collective-permute-start = (bf16[1552,128]{1,0:T(8,128)(2,1)S(1)}, bf16[1552,128]{1,0:T(8,128)(2,1)S(1)}, u32[]{:S(2)}, u32[]{:S(2)}) collective-permute-start(bf16[1552,128]{1,0:T(8,128)(2,1)S(1)} %get-tuple-element.21.c0), channel_id=1, source_target_pairs={{0,128},{128,256},{256,384},{384,0},{1,129},{129,257},{257,385},{3... | collective-permute-start | bytes 1191944 | tf_op jit(solution)/shard_map/ppermute | solution.py:218
  27.1 13.7 %all-reduce.5 = s32[16]{0:T(128)S(1)} all-reduce(s32[16]{0:T(128)S(1)} %dynamic-update-slice), channel_id=1, replica_groups=mesh['sec'=4,'zl'=4,'x'=4,'y'=4,'core'=2] {'x','y'}, use_global_device_ids=true, to_apply=%add.5 | all-reduce | flops 16 | bytes 128
  41.0 2.0 %shard_map.112 = (bf16[1024,192]{1,0:T(8,128)(2,1)S(1)}, bf16[1024,192]{1,0:T(8,128)(2,1)S(1)}, f32[64,64]{1,0:T(8,128)S(1)}) custom-call(s32[1]{0:T(128)} %bitcast.place, bf16[64,3072]{1,0:T(8,128)(2,1)S(1)} %copy-done.7, bf16[256,3072]{1,0:T(8,128)(2,1)S(1)} %copy-done, f32[16,256]{1,0:T(8,128)S(1)} %pad_maximum_fusion.1.temb), custom_call_target="tpu_custom_call" | custom-call | flops 1000 | bytes 30 | tf_op jit(solution)/shard_map/pallas_call | solution.py:251
  45.2 6.7 %all-to-all-done = bf16[8,3,24,384]{3,2,1,0:T(8,128)(2,1)} async-done(((bf16[8,3,24,384]{3,2,1,0:T(8,128)(2,1)}), bf16[8,3,24,384]{3,2,1,0:T(8,128)(2,1)}, u32[]{:S(2)}, u32[]{:S(2)}) %all-to-all-start) | async-done | bytes 442400 | tf_op jit(solution)/shard_map/all_to_all | solution.py:241
  54.0 3.2 %shard_map.113 = bf16[1024,1152]{1,0:T(8,128)(2,1)} custom-call(bf16[1024,192]{1,0:T(8,128)(2,1)S(1)} %copy-done.2, bf16[1024,192]{1,0:T(8,128)(2,1)S(1)} %copy-done.4, bf16[3,192,384]{2,1,0:T(8,128)(2,1)S(1)} %bitcast.48), custom_call_target="tpu_custom_call" | custom-call | flops 1000 | bytes 50 | tf_op jit(solution)/shard_map/pallas_call | solution.py:263
  58.6 3.3 %collective-permute-start.2 = (bf16[3,1,130,256]{3,2,1,0:T(8,128)(2,1)S(1)}, bf16[3,1,130,256]{3,2,1,0:T(8,128)(2,1)S(1)}, u32[]{:S(2)}, u32[]{:S(2)}) collective-permute-start(bf16[3,1,130,256]{3,2,1,0:T(8,128)(2,1)S(1)} %pad_maximum_fusion.v0), channel_id=1, source_target_pairs={{0,1},{1,2},{2,3},{3,4},{4,5},{5,6},{6,7},{7,8},{8,9},{9,10},{10,1... | collective-permute-start | bytes 599048 | tf_op jit(solution)/shard_map/ppermute | solution.py:218
  62.6 3.1 %collective-permute-done.2.v1 = bf16[3,1,130,256]{3,2,1,0:T(8,128)(2,1)S(1)} collective-permute-done((bf16[3,1,130,256]{3,2,1,0:T(8,128)(2,1)S(1)}, bf16[3,1,130,256]{3,2,1,0:T(8,128)(2,1)S(1)}, u32[]{:S(2)}, u32[]{:S(2)}) %collective-permute-start.2) | collective-permute-done | bytes 199712 | tf_op jit(solution)/shard_map/ppermute | solution.py:218
  66.5 13.9 %all-to-all-start.1 = ((bf16[16,64,1152]{2,1,0:T(8,128)(2,1)}), bf16[16,64,1152]{2,1,0:T(8,128)(2,1)S(1)}, u32[]{:S(2)}, u32[]{:S(2)}) async-start(bf16[16,64,1152]{2,1,0:T(8,128)(2,1)} %bitcast.17), calls=%async_computation.1 | async-start | bytes 4718592 | tf_op jit(solution)/shard_map/all_to_all | solution.py:301
  84.2 5.2 %collective-permute-start.5 = (bf16[768,128]{1,0:T(8,128)(2,1)S(1)}, bf16[768,128]{1,0:T(8,128)(2,1)S(1)}, u32[]{:S(2)}, u32[]{:S(2)}) collective-permute-start(bf16[768,128]{1,0:T(8,128)(2,1)S(1)} %slice.41), channel_id=1, source_target_pairs={{0,384},{128,0},{256,128},{384,256},{1,385},{129,1},{257,129},{385... | collective-permute-start | bytes 589832 | tf_op jit(solution)/shard_map/ppermute | solution.py:218
  89.4 4.0 %collective-permute-start.4 = (bf16[768,128]{1,0:T(8,128)(2,1)S(1)}, bf16[768,128]{1,0:T(8,128)(2,1)S(1)}, u32[]{:S(2)}, u32[]{:S(2)}) collective-permute-start(bf16[768,128]{1,0:T(8,128)(2,1)S(1)} %slice.40), channel_id=1, source_target_pairs={{0,128},{128,256},{256,384},{384,0},{1,129},{129,257},{257,385},{3... | collective-permute-start | bytes 589832 | tf_op jit(solution)/shard_map/ppermute | solution.py:218
  96.4 6.5 %shard_map.115 = (bf16[256,32]{1,0:T(8,128)(2,1)S(1)}, bf16[64,128]{1,0:T(8,128)(2,1)S(1)}) custom-call(f32[1]{0:T(128)S(6)} %div.9.level, bf16[3,1,130,256]{3,2,1,0:T(8,128)(2,1)S(1)} %copy-done.10, bf16[3,1,130,256]{3,2,1,0:T(8,128)(2,1)S(1)} %copy-done.12, bf16[3,1,130,256]{3,2,1,0:T(8,128)(2,1)S(1)} %pad_maximum_fusion.v0, ...), custom_call_target="tpu_custom_call" | custom-call | flops 10000 | bytes 10 | tf_op jit(solution)/shard_map/pallas_call | solution.py:282
  104.3 19.0 %all-gather = bf16[256,128]{1,0:T(8,128)(2,1)S(1)} all-gather(bf16[64,128]{1,0:T(8,128)(2,1)S(1)} %get-tuple-element.30), channel_id=2, replica_groups=mesh['sec'=4,'zl'=4,'x'=4,'y'=4,'core'=2] {'sec'}, dimensions={0}, use_global_device_ids=true | all-gather | bytes 81920 | tf_op jit(solution)/shard_map/all_gather | solution.py:302
  123.3 3.5 %shard_map.116.att = bf16[512,384]{1,0:T(8,128)(2,1)} custom-call(bf16[4,64,128]{2,1,0:T(8,128)(2,1)S(1)} %bitcast.51, bf16[16,64,1152]{2,1,0:T(8,128)(2,1)S(1)} %all-to-all-done.1.parts, f32[64,64]{1,0:T(8,128)S(1)} %copy-done.18), custom_call_target="tpu_custom_call" | custom-call | flops 4000 | bytes 10 | tf_op jit(solution)/shard_map/pallas_call | solution.py:303
  126.8 2.5 %shard_map.117 = bf16[8,192,384]{2,1,0:T(8,128)(2,1)S(1)} custom-call(s32[3]{0:T(128)S(1)} %pad_add_fusion.place, bf16[512,384]{1,0:T(8,128)(2,1)} %shard_map.116.att, bf16[1552,128]{1,0:T(8,128)(2,1)S(1)} %copy-done.6, bf16[1552,128]{1,0:T(8,128)(2,1)S(1)} %collective-permute-done.c_up, bf16[1552,128]{1,0:T(8,128)(2,1)S(1)} %collective-permute-done.1.c_down, ...), custom_call_target="tpu_custom_call" | custom-call | flops 1000 | bytes 50 | tf_op jit(solution)/shard_map/pallas_call | solution.py:308
  129.3 4.9 %collective-permute-start.6 = (bf16[4,192,384]{2,1,0:T(8,128)(2,1)S(1)}, bf16[4,192,384]{2,1,0:T(8,128)(2,1)S(1)}, u32[]{:S(2)}, u32[]{:S(2)}) collective-permute-start(bf16[4,192,384]{2,1,0:T(8,128)(2,1)S(1)} %slice.49), channel_id=1, source_target_pairs={{0,1},{1,0},{2,3},{3,2},{4,5},{5,4},{6,7},{7,6},{8,9},{9,8},{10,11... | collective-permute-start | bytes 1769480 | tf_op jit(solution)/shard_map/ppermute | solution.py:218
  134.3 6.4 %all-to-all-start.2 = ((bf16[4,128,384]{2,1,0:T(8,128)(2,1)}), bf16[4,128,384]{2,1,0:T(8,128)(2,1)S(1)}, u32[]{:S(2)}, u32[]{:S(2)}) async-start(bf16[4,128,384]{2,1,0:T(8,128)(2,1)} %bitcast.18), calls=%async_computation.2 | async-start | bytes 786432 | tf_op jit(solution)/shard_map/all_to_all | solution.py:306
  140.9 3.3 %collective-permute-start.7 = (bf16[192,384]{1,0:T(8,128)(2,1)S(1)}, bf16[192,384]{1,0:T(8,128)(2,1)S(1)}, u32[]{:S(2)}, u32[]{:S(2)}) collective-permute-start(bf16[192,384]{1,0:T(8,128)(2,1)S(1)} %get-tuple-element.37), channel_id=1, source_target_pairs={{0,2},{2,4},{4,6},{6,0},{1,3},{3,5},{5,7},{7,1},{8,10},{10,12},{12... | collective-permute-start | bytes 442376 | tf_op jit(solution)/shard_map/ppermute | solution.py:218
  144.2 3.2 %collective-permute-start.9 = (bf16[192,384]{1,0:T(8,128)(2,1)S(1)}, bf16[192,384]{1,0:T(8,128)(2,1)S(1)}, u32[]{:S(2)}, u32[]{:S(2)}) collective-permute-start(bf16[192,384]{1,0:T(8,128)(2,1)S(1)} %get-tuple-element.38), channel_id=1, source_target_pairs={{0,6},{2,0},{4,2},{6,4},{1,7},{3,1},{5,3},{7,5},{8,14},{10,8},{12,... | collective-permute-start | bytes 442376 | tf_op jit(solution)/shard_map/ppermute | solution.py:218
  147.4 3.6 %collective-permute-start.8 = (bf16[192,384]{1,0:T(8,128)(2,1)S(1)}, bf16[192,384]{1,0:T(8,128)(2,1)S(1)}, u32[]{:S(2)}, u32[]{:S(2)}) collective-permute-start(bf16[192,384]{1,0:T(8,128)(2,1)S(1)} %get-tuple-element.39), channel_id=1, source_target_pairs={{0,4},{2,6},{4,0},{6,2},{1,5},{3,7},{5,1},{7,3},{8,12},{10,14},{12... | collective-permute-start | bytes 442376 | tf_op jit(solution)/shard_map/ppermute | solution.py:218
  151.0 4.3 %collective-permute-done.8 = bf16[192,384]{1,0:T(8,128)(2,1)S(1)} collective-permute-done((bf16[192,384]{1,0:T(8,128)(2,1)S(1)}, bf16[192,384]{1,0:T(8,128)(2,1)S(1)}, u32[]{:S(2)}, u32[]{:S(2)}) %collective-permute-start.8) | collective-permute-done | bytes 147488 | tf_op jit(solution)/shard_map/ppermute | solution.py:218
  156.2 16.6 %all-to-all-start.3 = ((bf16[16,12,384]{2,1,0:T(8,128)(2,1)}), bf16[16,12,384]{2,1,0:T(8,128)(2,1)S(1)}, u32[]{:S(2)}, u32[]{:S(2)}) async-start(bf16[16,12,384]{2,1,0:T(8,128)(2,1)} %reshape.65), calls=%async_computation.3 | async-start | bytes 393216 | tf_op jit(solution)/shard_map/all_to_all | solution.py:329
  174.7 6.5 %all-to-all-done.3 = bf16[16,12,384]{2,1,0:T(8,128)(2,1)S(1)} async-done(((bf16[16,12,384]{2,1,0:T(8,128)(2,1)}), bf16[16,12,384]{2,1,0:T(8,128)(2,1)S(1)}, u32[]{:S(2)}, u32[]{:S(2)}) %all-to-all-start.3) | async-done | bytes 147488 | tf_op jit(solution)/shard_map/all_to_all | solution.py:329
  (98 shorter events, 24.7 us)
Async XLA Ops:
  0.6 13.5 %copy-start.19 = (bf16[1,128,1536]{2,1,0:T(8,128)(2,1)S(1)}, bf16[1,128,1536]{2,1,0:T(8,128)(2,1)}, u32[]{:S(2)}) copy-start(bf16[1,128,1536]{2,1,0:T(8,128)(2,1)} %param.17) | copy-start | bytes 1179652
  2.3 38.6 %copy-start = (bf16[256,3072]{1,0:T(8,128)(2,1)S(1)}, bf16[256,3072]{1,0:T(8,128)(2,1)}, u32[]{:S(2)}) copy-start(bf16[256,3072]{1,0:T(8,128)(2,1)} %mod.1) | copy-start | bytes 4718596
  2.3 38.6 %copy-start.7 = (bf16[64,3072]{1,0:T(8,128)(2,1)S(1)}, bf16[64,3072]{1,0:T(8,128)(2,1)}, u32[]{:S(2)}) copy-start(bf16[64,3072]{1,0:T(8,128)(2,1)} %embed.1) | copy-start | bytes 1179652
  2.3 49.5 %all-to-all-start = ((bf16[8,3,24,384]{3,2,1,0:T(8,128)(2,1)}), bf16[8,3,24,384]{3,2,1,0:T(8,128)(2,1)}, u32[]{:S(2)}, u32[]{:S(2)}) async-start(bf16[8,3,24,384]{3,2,1,0:T(8,128)(2,1)} %broadcast_in_dim.23), calls=%async_computation | async-start | bytes 884736 | tf_op jit(solution)/shard_map/all_to_all | solution.py:241
  15.2 37.7 %copy-start.5 = (bf16[1552,128]{1,0:T(8,128)(2,1)}, bf16[1552,128]{1,0:T(8,128)(2,1)S(1)}, u32[]{:S(2)}) copy-start(bf16[1552,128]{1,0:T(8,128)(2,1)S(1)} %get-tuple-element.21.c0) | copy-start | bytes 1191940
  15.2 42.0 %collective-permute-start.1 = (bf16[1552,128]{1,0:T(8,128)(2,1)}, bf16[1552,128]{1,0:T(8,128)(2,1)S(1)}, u32[]{:S(2)}, u32[]{:S(2)}) collective-permute-start(bf16[1552,128]{1,0:T(8,128)(2,1)} %get-tuple-element.22), channel_id=1, source_target_pairs={{0,384},{128,0},{256,128},{384,256},{1,385},{129,1},{257,129},{385... | collective-permute-start | bytes 1191944 | tf_op jit(solution)/shard_map/ppermute | solution.py:218
  25.0 32.2 %collective-permute-start = (bf16[1552,128]{1,0:T(8,128)(2,1)S(1)}, bf16[1552,128]{1,0:T(8,128)(2,1)S(1)}, u32[]{:S(2)}, u32[]{:S(2)}) collective-permute-start(bf16[1552,128]{1,0:T(8,128)(2,1)S(1)} %get-tuple-element.21.c0), channel_id=1, source_target_pairs={{0,128},{128,256},{256,384},{384,0},{1,129},{129,257},{257,385},{3... | collective-permute-start | bytes 1191944 | tf_op jit(solution)/shard_map/ppermute | solution.py:218
  45.2 7.8 %copy-start.2 = (bf16[1024,192]{1,0:T(8,128)(2,1)S(1)}, bf16[1024,192]{1,0:T(8,128)(2,1)}, u32[]{:S(2)}) copy-start(bf16[1024,192]{1,0:T(8,128)(2,1)} %copy-done.1) | copy-start | bytes 1179652
  57.3 4.7 %collective-permute-start.3 = (bf16[3,1,130,256]{3,2,1,0:T(8,128)(2,1)S(1)}, bf16[3,1,130,256]{3,2,1,0:T(8,128)(2,1)S(1)}, u32[]{:S(2)}, u32[]{:S(2)}) collective-permute-start(bf16[3,1,130,256]{3,2,1,0:T(8,128)(2,1)S(1)} %pad_maximum_fusion.v0), channel_id=1, source_target_pairs={{0,2},{1,3},{2,4},{3,5},{4,6},{5,7},{6,8},{7,9},{8,10},{9,11},{10,... | collective-permute-start | bytes 599048 | tf_op jit(solution)/shard_map/ppermute | solution.py:218
  58.6 7.2 %collective-permute-start.2 = (bf16[3,1,130,256]{3,2,1,0:T(8,128)(2,1)S(1)}, bf16[3,1,130,256]{3,2,1,0:T(8,128)(2,1)S(1)}, u32[]{:S(2)}, u32[]{:S(2)}) collective-permute-start(bf16[3,1,130,256]{3,2,1,0:T(8,128)(2,1)S(1)} %pad_maximum_fusion.v0), channel_id=1, source_target_pairs={{0,1},{1,2},{2,3},{3,4},{4,5},{5,6},{6,7},{7,8},{8,9},{9,10},{10,1... | collective-permute-start | bytes 599048 | tf_op jit(solution)/shard_map/ppermute | solution.py:218
  66.4 13.9 %copy-start.22 = (bf16[128,81]{0,1:T(8,128)(2,1)S(1)}, bf16[128,81]{0,1:T(8,128)(2,1)}, u32[]{:S(2)}) copy-start(bf16[128,81]{0,1:T(8,128)(2,1)} %param.10) | copy-start | bytes 62212
  66.5 14.1 %copy-start.21 = (bf16[16,1,16,32]{3,2,1,0:T(8,128)(2,1)S(1)}, bf16[16,1,16,32]{3,2,1,0:T(8,128)(2,1)}, u32[]{:S(2)}) copy-start(bf16[16,1,16,32]{3,2,1,0:T(8,128)(2,1)} %param.12) | copy-start | bytes 49156
  66.5 56.8 %all-to-all-start.1 = ((bf16[16,64,1152]{2,1,0:T(8,128)(2,1)}), bf16[16,64,1152]{2,1,0:T(8,128)(2,1)S(1)}, u32[]{:S(2)}, u32[]{:S(2)}) async-start(bf16[16,64,1152]{2,1,0:T(8,128)(2,1)} %bitcast.17), calls=%async_computation.1 | async-start | bytes 4718592 | tf_op jit(solution)/shard_map/all_to_all | solution.py:301
  81.4 41.9 %copy-start.18 = (f32[64,64]{1,0:T(8,128)S(1)}, f32[64,64]{1,0:T(8,128)}, u32[]{:S(2)}) copy-start(f32[64,64]{1,0:T(8,128)} %copy-done.17) | copy-start | bytes 49156
  84.2 18.7 %collective-permute-start.5 = (bf16[768,128]{1,0:T(8,128)(2,1)S(1)}, bf16[768,128]{1,0:T(8,128)(2,1)S(1)}, u32[]{:S(2)}, u32[]{:S(2)}) collective-permute-start(bf16[768,128]{1,0:T(8,128)(2,1)S(1)} %slice.41), channel_id=1, source_target_pairs={{0,384},{128,0},{256,128},{384,256},{1,385},{129,1},{257,129},{385... | collective-permute-start | bytes 589832 | tf_op jit(solution)/shard_map/ppermute | solution.py:218
  89.4 14.2 %collective-permute-start.4 = (bf16[768,128]{1,0:T(8,128)(2,1)S(1)}, bf16[768,128]{1,0:T(8,128)(2,1)S(1)}, u32[]{:S(2)}, u32[]{:S(2)}) collective-permute-start(bf16[768,128]{1,0:T(8,128)(2,1)S(1)} %slice.40), channel_id=1, source_target_pairs={{0,128},{128,256},{256,384},{384,0},{1,129},{129,257},{257,385},{3... | collective-permute-start | bytes 589832 | tf_op jit(solution)/shard_map/ppermute | solution.py:218
  123.3 3.5 %copy-start.6 = (bf16[1552,128]{1,0:T(8,128)(2,1)S(1)}, bf16[1552,128]{1,0:T(8,128)(2,1)}, u32[]{:S(2)}) copy-start(bf16[1552,128]{1,0:T(8,128)(2,1)} %copy-done.5) | copy-start | bytes 1191940
  123.3 3.5 %copy-start.14 = (bf16[768,128]{1,0:T(8,128)(2,1)S(1)}, bf16[768,128]{1,0:T(8,128)(2,1)}, u32[]{:S(2)}) copy-start(bf16[768,128]{1,0:T(8,128)(2,1)} %copy-done.13) | copy-start | bytes 589828
  129.3 11.3 %collective-permute-start.6 = (bf16[4,192,384]{2,1,0:T(8,128)(2,1)S(1)}, bf16[4,192,384]{2,1,0:T(8,128)(2,1)S(1)}, u32[]{:S(2)}, u32[]{:S(2)}) collective-permute-start(bf16[4,192,384]{2,1,0:T(8,128)(2,1)S(1)} %slice.49), channel_id=1, source_target_pairs={{0,1},{1,0},{2,3},{3,2},{4,5},{5,4},{6,7},{7,6},{8,9},{9,8},{10,11... | collective-permute-start | bytes 1769480 | tf_op jit(solution)/shard_map/ppermute | solution.py:218
  134.3 22.0 %all-to-all-start.2 = ((bf16[4,128,384]{2,1,0:T(8,128)(2,1)}), bf16[4,128,384]{2,1,0:T(8,128)(2,1)S(1)}, u32[]{:S(2)}, u32[]{:S(2)}) async-start(bf16[4,128,384]{2,1,0:T(8,128)(2,1)} %bitcast.18), calls=%async_computation.2 | async-start | bytes 786432 | tf_op jit(solution)/shard_map/all_to_all | solution.py:306
  140.9 10.1 %collective-permute-start.7 = (bf16[192,384]{1,0:T(8,128)(2,1)S(1)}, bf16[192,384]{1,0:T(8,128)(2,1)S(1)}, u32[]{:S(2)}, u32[]{:S(2)}) collective-permute-start(bf16[192,384]{1,0:T(8,128)(2,1)S(1)} %get-tuple-element.37), channel_id=1, source_target_pairs={{0,2},{2,4},{4,6},{6,0},{1,3},{3,5},{5,7},{7,1},{8,10},{10,12},{12... | collective-permute-start | bytes 442376 | tf_op jit(solution)/shard_map/ppermute | solution.py:218
  144.2 6.8 %collective-permute-start.9 = (bf16[192,384]{1,0:T(8,128)(2,1)S(1)}, bf16[192,384]{1,0:T(8,128)(2,1)S(1)}, u32[]{:S(2)}, u32[]{:S(2)}) collective-permute-start(bf16[192,384]{1,0:T(8,128)(2,1)S(1)} %get-tuple-element.38), channel_id=1, source_target_pairs={{0,6},{2,0},{4,2},{6,4},{1,7},{3,1},{5,3},{7,5},{8,14},{10,8},{12,... | collective-permute-start | bytes 442376 | tf_op jit(solution)/shard_map/ppermute | solution.py:218
  147.4 7.9 %collective-permute-start.8 = (bf16[192,384]{1,0:T(8,128)(2,1)S(1)}, bf16[192,384]{1,0:T(8,128)(2,1)S(1)}, u32[]{:S(2)}, u32[]{:S(2)}) collective-permute-start(bf16[192,384]{1,0:T(8,128)(2,1)S(1)} %get-tuple-element.39), channel_id=1, source_target_pairs={{0,4},{2,6},{4,0},{6,2},{1,5},{3,7},{5,1},{7,3},{8,12},{10,14},{12... | collective-permute-start | bytes 442376 | tf_op jit(solution)/shard_map/ppermute | solution.py:218
  156.2 24.9 %all-to-all-start.3 = ((bf16[16,12,384]{2,1,0:T(8,128)(2,1)}), bf16[16,12,384]{2,1,0:T(8,128)(2,1)S(1)}, u32[]{:S(2)}, u32[]{:S(2)}) async-start(bf16[16,12,384]{2,1,0:T(8,128)(2,1)} %reshape.65), calls=%async_computation.3 | async-start | bytes 393216 | tf_op jit(solution)/shard_map/all_to_all | solution.py:329
  (13 other events, 15.5 us)

commit v4 on v3

--- a/solution.py
+++ b/solution.py
@@ -80,7 +80,7 @@
         a_lo[64 * f : 64 * f + 64] = (a - hi.astype(F32)).astype(BF16)
 
 
-def fold_body(a_hi, a_lo, w, out):
+def fold_body(a_hi, a_lo, w, noise, conv, out):
     for h in range(3):
         prod = jnp.dot(a_hi[...], w[h], preferred_element_type=F32) + jnp.dot(
             a_lo[...], w[h], preferred_element_type=F32
@@ -260,9 +260,15 @@
         10**9,
         3 * 10**6,
     )(place, embed_weight, mod_weight, temb)
+    taps = conv_weight.reshape(128, 3, 3, 3, 3).transpose(0, 3, 4, 1, 2).reshape(128, 3, 27)
+    taps = jnp.pad(taps, ((0, 0), (0, 0), (0, 5))).reshape(128, 96)
+    conv = jnp.concatenate(
+        [jnp.pad(taps, ((0, 0), (0, 32))), jnp.pad(taps, ((0, 0), (32, 0)))], axis=0
+    )
+    noise_t = noise.reshape(16, 8, 2, 16, 2).transpose(4, 2, 0, 1, 3).reshape(64, 128)
     partial = call(
-        fold_body, jax.ShapeDtypeStruct((1024, 1152), BF16), 0, 3, 10**9, 5 * 10**6
-    )(a_hi, a_lo, rows)
+        fold_body, jax.ShapeDtypeStruct((1024, 1152), BF16), 0, 3, 10**9, 5 * 10**6, (), 2
+    )(a_hi, a_lo, rows, noise_t, conv)
     partial, c_up, c_down = together(partial, c_up, c_down)
     sec = lax.axis_index("sec").astype(jnp.int32)[None]
     above = jnp.where(sec[0] == 0, 0, c_up[1536:1542]).astype(BF16).reshape(3, 1, 1, 256)
@@ -271,13 +277,7 @@
     v1, v2 = moved(v0, SEQ, 128, 1, False), moved(v0, SEQ, 128, 2, False)
     partial, v1, v2 = together(partial, v1, v2)
 
-    taps = conv_weight.reshape(128, 3, 3, 3, 3).transpose(0, 3, 4, 1, 2).reshape(128, 3, 27)
-    taps = jnp.pad(taps, ((0, 0), (0, 0), (0, 5))).reshape(128, 96)
-    conv = jnp.concatenate(
-        [jnp.pad(taps, ((0, 0), (0, 32))), jnp.pad(taps, ((0, 0), (32, 0)))], axis=0
-    )
     down = down_weight.transpose(1, 2, 3, 0).reshape(8, 128, 128)
-    noise_t = noise.reshape(16, 8, 2, 16, 2).transpose(4, 2, 0, 1, 3).reshape(64, 128)
     level = (timesteps.astype(F32) + 1.0) / STEPS
     lat, pat = call(
         encode_body,

time: 184 us -> 182 us (0.989)
  local copies, waits for them, and re-layouts: 21.1 us -> 16.3 us
  waiting for transfers between devices: 20.9 us -> 23.3 us
  starting transfers between devices: 85.8 us -> 88.1 us
    unnamed x51 -> x35, local copies, waits for them, and re-layouts: 11.8 us -> 8.21 us
    ppermute x10, waiting for transfers between devices: 7.52 us -> 10.5 us  [moved(): return lax.ppermute(shard, axis, pairs)]
    ppermute x10, starting transfers between devices: 38 us -> 40.8 us  [moved(): return lax.ppermute(shard, axis, pairs)]
  transfers between devices with their start and end apart: 14 -> 14, of which waited for: 6 -> 5; matrix products, arithmetic and copies ran while one was open for 6% -> 5% of each run, Pallas kernels for 7% -> 7%
where the time goes in v4:
time: 182 us; the launch traced here: 181 us
  starting transfers between devices  88.1 us (48%)
  blocking collectives  31.6 us (17%)
  waiting for transfers between devices  23.3 us (13%)
  Pallas kernels  18.8 us (10%)
  local copies, waits for them, and re-layouts  16.3 us (9%)
    ppermute x10, starting transfers between devices, moved(): return lax.ppermute(shard, axis, pairs)  40.8 us
    all_gather x1, blocking collectives, on_device(): pats = lax.all_gather(pat, 'sec', axis=0)  17.7 us
    all_to_all x1, starting transfers between devices, on_device(): lax.all_to_all(row_sum.reshape(16, 12, 384), ('zl', 'x'), 0, 0, tiled=True)  17.1 us
    unnamed x1, blocking collectives  13.9 us
    all_to_all x1, starting transfers between devices, on_device(): lax.all_to_all(partial.reshape(16, 64, 1152), ('x', 'y'), 0, 0, tiled=True)  12.7 us
    all_to_all x1, starting transfers between devices, on_device(): lax.all_to_all(jnp.broadcast_to(qkv_weight.transpose(1, 0, 2), (8, 3, 24,...  11 us
    ppermute x10, waiting for transfers between devices, moved(): return lax.ppermute(shard, axis, pairs)  10.5 us
    unnamed x35, local copies, waits for them, and re-layouts  8.21 us
  transfers between devices with their start and end apart: 14, of which 5 were waited for; matrix products, arithmetic and copies ran while one was open for 5% of the time, Pallas kernels for 7%

profile of v4, /device:TPU:1, one launch (start us, length us, event | category | flops | bytes accessed | tf_op | source)
XLA Modules:
  0.0 181.1 jit_solution(11689524477203997748)
XLA Ops:
  2.3 11.0 %all-to-all-start = ((bf16[8,3,24,384]{3,2,1,0:T(8,128)(2,1)}), bf16[8,3,24,384]{3,2,1,0:T(8,128)(2,1)}, u32[]{:S(2)}, u32[]{:S(2)}) async-start(bf16[8,3,24,384]{3,2,1,0:T(8,128)(2,1)} %broadcast_in_dim.23), calls=%async_computation | async-start | bytes 884736 | tf_op jit(solution)/shard_map/all_to_all | solution.py:241
  15.4 7.2 %collective-permute-start.1 = (bf16[1552,128]{1,0:T(8,128)(2,1)}, bf16[1552,128]{1,0:T(8,128)(2,1)S(1)}, u32[]{:S(2)}, u32[]{:S(2)}) collective-permute-start(bf16[1552,128]{1,0:T(8,128)(2,1)} %get-tuple-element.22), channel_id=1, source_target_pairs={{0,384},{128,0},{256,128},{384,256},{1,385},{129,1},{257,129},{385... | collective-permute-start | bytes 1191944 | tf_op jit(solution)/shard_map/ppermute | solution.py:218
  25.3 2.1 %collective-permute-start = (bf16[1552,128]{1,0:T(8,128)(2,1)}, bf16[1552,128]{1,0:T(8,128)(2,1)S(1)}, u32[]{:S(2)}, u32[]{:S(2)}) collective-permute-start(bf16[1552,128]{1,0:T(8,128)(2,1)} %get-tuple-element.21.c0), channel_id=1, source_target_pairs={{0,128},{128,256},{256,384},{384,0},{1,129},{129,257},{257,385},{3... | collective-permute-start | bytes 1191944 | tf_op jit(solution)/shard_map/ppermute | solution.py:218
  27.4 13.9 %all-reduce.5 = s32[16]{0:T(128)S(1)} all-reduce(s32[16]{0:T(128)S(1)} %dynamic-update-slice), channel_id=1, replica_groups=mesh['sec'=4,'zl'=4,'x'=4,'y'=4,'core'=2] {'x','y'}, use_global_device_ids=true, to_apply=%add.5 | all-reduce | flops 16 | bytes 128
  41.5 2.0 %shard_map.112 = (bf16[1024,192]{1,0:T(8,128)(2,1)S(1)}, bf16[1024,192]{1,0:T(8,128)(2,1)S(1)}, f32[64,64]{1,0:T(8,128)S(1)}) custom-call(s32[1]{0:T(128)} %bitcast.place, bf16[64,3072]{1,0:T(8,128)(2,1)S(1)} %copy-done.5, bf16[256,3072]{1,0:T(8,128)(2,1)S(1)} %copy-done, f32[16,256]{1,0:T(8,128)S(1)} %pad_maximum_fusion.1.temb), custom_call_target="tpu_custom_call" | custom-call | flops 1000 | bytes 30 | tf_op jit(solution)/shard_map/pallas_call | solution.py:251
  45.8 6.0 %all-to-all-done = bf16[8,3,24,384]{3,2,1,0:T(8,128)(2,1)} async-done(((bf16[8,3,24,384]{3,2,1,0:T(8,128)(2,1)}), bf16[8,3,24,384]{3,2,1,0:T(8,128)(2,1)}, u32[]{:S(2)}, u32[]{:S(2)}) %all-to-all-start) | async-done | bytes 442400 | tf_op jit(solution)/shard_map/all_to_all | solution.py:241
  52.9 3.2 %shard_map.113 = bf16[1024,1152]{1,0:T(8,128)(2,1)} custom-call(bf16[1024,192]{1,0:T(8,128)(2,1)S(1)} %copy-done.2, bf16[1024,192]{1,0:T(8,128)(2,1)S(1)} %copy-done.4, bf16[3,192,384]{2,1,0:T(8,128)(2,1)S(1)} %bitcast.48, bf16[64,128]{1,0:T(8,128)(2,1)S(1)} %reshape.56.noise, bf16[256,128]{1,0:T(8,128)(2,1)S(1)} %fusion.5.conv), custom_call_target="tpu_custom_call" | custom-call | flops 1000 | bytes 50 | tf_op jit(solution)/shard_map/pallas_call | solution.py:269
  57.5 7.1 %collective-permute-start.2 = (bf16[3,1,130,256]{3,2,1,0:T(8,128)(2,1)S(1)}, bf16[3,1,130,256]{3,2,1,0:T(8,128)(2,1)S(1)}, u32[]{:S(2)}, u32[]{:S(2)}) collective-permute-start(bf16[3,1,130,256]{3,2,1,0:T(8,128)(2,1)S(1)} %pad_maximum_fusion.v0), channel_id=1, source_target_pairs={{0,1},{1,2},{2,3},{3,4},{4,5},{5,6},{6,7},{7,8},{8,9},{9,10},{10,1... | collective-permute-start | bytes 599048 | tf_op jit(solution)/shard_map/ppermute | solution.py:218
  65.3 2.0 %collective-permute-done.2.v1 = bf16[3,1,130,256]{3,2,1,0:T(8,128)(2,1)S(1)} collective-permute-done((bf16[3,1,130,256]{3,2,1,0:T(8,128)(2,1)S(1)}, bf16[3,1,130,256]{3,2,1,0:T(8,128)(2,1)S(1)}, u32[]{:S(2)}, u32[]{:S(2)}) %collective-permute-start.2) | collective-permute-done | bytes 199712 | tf_op jit(solution)/shard_map/ppermute | solution.py:218
  68.0 12.7 %all-to-all-start.1 = ((bf16[16,64,1152]{2,1,0:T(8,128)(2,1)}), bf16[16,64,1152]{2,1,0:T(8,128)(2,1)S(1)}, u32[]{:S(2)}, u32[]{:S(2)}) async-start(bf16[16,64,1152]{2,1,0:T(8,128)(2,1)} %bitcast.17), calls=%async_computation.1 | async-start | bytes 4718592 | tf_op jit(solution)/shard_map/all_to_all | solution.py:301
  82.1 5.2 %collective-permute-start.5 = (bf16[768,128]{1,0:T(8,128)(2,1)}, bf16[768,128]{1,0:T(8,128)(2,1)}, u32[]{:S(2)}, u32[]{:S(2)}) collective-permute-start(bf16[768,128]{1,0:T(8,128)(2,1)} %slice.41), channel_id=1, source_target_pairs={{0,384},{128,0},{256,128},{384,256},{1,385},{129,1},{257,129},{385... | collective-permute-start | bytes 589832 | tf_op jit(solution)/shard_map/ppermute | solution.py:218
  87.3 4.0 %collective-permute-start.4 = (bf16[768,128]{1,0:T(8,128)(2,1)}, bf16[768,128]{1,0:T(8,128)(2,1)}, u32[]{:S(2)}, u32[]{:S(2)}) collective-permute-start(bf16[768,128]{1,0:T(8,128)(2,1)} %slice.40), channel_id=1, source_target_pairs={{0,128},{128,256},{256,384},{384,0},{1,129},{129,257},{257,385},{3... | collective-permute-start | bytes 589832 | tf_op jit(solution)/shard_map/ppermute | solution.py:218
  94.2 6.5 %shard_map.115 = (bf16[256,32]{1,0:T(8,128)(2,1)S(1)}, bf16[64,128]{1,0:T(8,128)(2,1)S(1)}) custom-call(f32[1]{0:T(128)S(6)} %div.9.level, bf16[3,1,130,256]{3,2,1,0:T(8,128)(2,1)S(1)} %copy-done.8, bf16[3,1,130,256]{3,2,1,0:T(8,128)(2,1)S(1)} %copy-done.10, bf16[3,1,130,256]{3,2,1,0:T(8,128)(2,1)S(1)} %pad_maximum_fusion.v0, ...), custom_call_target="tpu_custom_call" | custom-call | flops 10000 | bytes 10 | tf_op jit(solution)/shard_map/pallas_call | solution.py:282
  100.7 3.9 %collective-permute-done.5.far_b = bf16[768,128]{1,0:T(8,128)(2,1)} collective-permute-done((bf16[768,128]{1,0:T(8,128)(2,1)}, bf16[768,128]{1,0:T(8,128)(2,1)}, u32[]{:S(2)}, u32[]{:S(2)}) %collective-permute-start.5) | collective-permute-done | bytes 196640 | tf_op jit(solution)/shard_map/ppermute | solution.py:218
  104.7 17.7 %all-gather = bf16[256,128]{1,0:T(8,128)(2,1)S(1)} all-gather(bf16[64,128]{1,0:T(8,128)(2,1)S(1)} %get-tuple-element.30), channel_id=2, replica_groups=mesh['sec'=4,'zl'=4,'x'=4,'y'=4,'core'=2] {'sec'}, dimensions={0}, use_global_device_ids=true | all-gather | bytes 81920 | tf_op jit(solution)/shard_map/all_gather | solution.py:302
  122.4 3.4 %shard_map.116.att = bf16[512,384]{1,0:T(8,128)(2,1)} custom-call(bf16[4,64,128]{2,1,0:T(8,128)(2,1)S(1)} %bitcast.51, bf16[16,64,1152]{2,1,0:T(8,128)(2,1)S(1)} %all-to-all-done.1.parts, f32[64,64]{1,0:T(8,128)S(1)} %get-tuple-element.32.gram), custom_call_target="tpu_custom_call" | custom-call | flops 4000 | bytes 10 | tf_op jit(solution)/shard_map/pallas_call | solution.py:303
  125.8 2.7 %shard_map.117 = bf16[8,192,384]{2,1,0:T(8,128)(2,1)S(1)} custom-call(s32[3]{0:T(128)S(1)} %pad_add_fusion.place, bf16[512,384]{1,0:T(8,128)(2,1)} %shard_map.116.att, bf16[1552,128]{1,0:T(8,128)(2,1)} %get-tuple-element.21.c0, bf16[1552,128]{1,0:T(8,128)(2,1)S(1)} %collective-permute-done.c_up, bf16[1552,128]{1,0:T(8,128)(2,1)S(1)} %collective-permute-done.1.c_down, ...), custom_call_target="tpu_custom_call" | custom-call | flops 1000 | bytes 50 | tf_op jit(solution)/shard_map/pallas_call | solution.py:308
  130.5 6.5 %all-to-all-start.2 = ((bf16[4,128,384]{2,1,0:T(8,128)(2,1)}), bf16[4,128,384]{2,1,0:T(8,128)(2,1)S(1)}, u32[]{:S(2)}, u32[]{:S(2)}) async-start(bf16[4,128,384]{2,1,0:T(8,128)(2,1)} %bitcast.18), calls=%async_computation.2 | async-start | bytes 786432 | tf_op jit(solution)/shard_map/all_to_all | solution.py:306
  137.2 5.2 %collective-permute-start.7 = (bf16[192,384]{1,0:T(8,128)(2,1)S(1)}, bf16[192,384]{1,0:T(8,128)(2,1)S(1)}, u32[]{:S(2)}, u32[]{:S(2)}) collective-permute-start(bf16[192,384]{1,0:T(8,128)(2,1)S(1)} %get-tuple-element.37), channel_id=1, source_target_pairs={{0,2},{2,4},{4,6},{6,0},{1,3},{3,5},{5,7},{7,1},{8,10},{10,12},{12... | collective-permute-start | bytes 442376 | tf_op jit(solution)/shard_map/ppermute | solution.py:218
  142.4 3.1 %collective-permute-start.9 = (bf16[192,384]{1,0:T(8,128)(2,1)S(1)}, bf16[192,384]{1,0:T(8,128)(2,1)S(1)}, u32[]{:S(2)}, u32[]{:S(2)}) collective-permute-start(bf16[192,384]{1,0:T(8,128)(2,1)S(1)} %get-tuple-element.38), channel_id=1, source_target_pairs={{0,6},{2,0},{4,2},{6,4},{1,7},{3,1},{5,3},{7,5},{8,14},{10,8},{12,... | collective-permute-start | bytes 442376 | tf_op jit(solution)/shard_map/ppermute | solution.py:218
  145.6 3.7 %collective-permute-start.8 = (bf16[192,384]{1,0:T(8,128)(2,1)S(1)}, bf16[192,384]{1,0:T(8,128)(2,1)S(1)}, u32[]{:S(2)}, u32[]{:S(2)}) collective-permute-start(bf16[192,384]{1,0:T(8,128)(2,1)S(1)} %get-tuple-element.39), channel_id=1, source_target_pairs={{0,4},{2,6},{4,0},{6,2},{1,5},{3,7},{5,1},{7,3},{8,12},{10,14},{12... | collective-permute-start | bytes 442376 | tf_op jit(solution)/shard_map/ppermute | solution.py:218
  149.3 4.5 %collective-permute-done.8 = bf16[192,384]{1,0:T(8,128)(2,1)S(1)} collective-permute-done((bf16[192,384]{1,0:T(8,128)(2,1)S(1)}, bf16[192,384]{1,0:T(8,128)(2,1)S(1)}, u32[]{:S(2)}, u32[]{:S(2)}) %collective-permute-start.8) | collective-permute-done | bytes 147488 | tf_op jit(solution)/shard_map/ppermute | solution.py:218
  154.6 17.1 %all-to-all-start.3 = ((bf16[16,12,384]{2,1,0:T(8,128)(2,1)}), bf16[16,12,384]{2,1,0:T(8,128)(2,1)S(1)}, u32[]{:S(2)}, u32[]{:S(2)}) async-start(bf16[16,12,384]{2,1,0:T(8,128)(2,1)} %reshape.65), calls=%async_computation.3 | async-start | bytes 393216 | tf_op jit(solution)/shard_map/all_to_all | solution.py:329
  173.6 6.8 %all-to-all-done.3 = bf16[16,12,384]{2,1,0:T(8,128)(2,1)S(1)} async-done(((bf16[16,12,384]{2,1,0:T(8,128)(2,1)}), bf16[16,12,384]{2,1,0:T(8,128)(2,1)S(1)}, u32[]{:S(2)}, u32[]{:S(2)}) %all-to-all-start.3) | async-done | bytes 147488 | tf_op jit(solution)/shard_map/all_to_all | solution.py:329
  (82 shorter events, 21.8 us)
Async XLA Ops:
  0.6 13.5 %copy-start.11 = (bf16[1,128,1536]{2,1,0:T(8,128)(2,1)S(1)}, bf16[1,128,1536]{2,1,0:T(8,128)(2,1)}, u32[]{:S(2)}) copy-start(bf16[1,128,1536]{2,1,0:T(8,128)(2,1)} %param.17) | copy-start | bytes 1179652
  2.3 39.1 %copy-start = (bf16[256,3072]{1,0:T(8,128)(2,1)S(1)}, bf16[256,3072]{1,0:T(8,128)(2,1)}, u32[]{:S(2)}) copy-start(bf16[256,3072]{1,0:T(8,128)(2,1)} %mod.1) | copy-start | bytes 4718596
  2.3 39.1 %copy-start.5 = (bf16[64,3072]{1,0:T(8,128)(2,1)S(1)}, bf16[64,3072]{1,0:T(8,128)(2,1)}, u32[]{:S(2)}) copy-start(bf16[64,3072]{1,0:T(8,128)(2,1)} %embed.1) | copy-start | bytes 1179652
  2.3 49.4 %all-to-all-start = ((bf16[8,3,24,384]{3,2,1,0:T(8,128)(2,1)}), bf16[8,3,24,384]{3,2,1,0:T(8,128)(2,1)}, u32[]{:S(2)}, u32[]{:S(2)}) async-start(bf16[8,3,24,384]{3,2,1,0:T(8,128)(2,1)} %broadcast_in_dim.23), calls=%async_computation | async-start | bytes 884736 | tf_op jit(solution)/shard_map/all_to_all | solution.py:241
  14.4 30.7 %copy-start.14 = (bf16[128,81]{0,1:T(8,128)(2,1)S(1)}, bf16[128,81]{0,1:T(8,128)(2,1)}, u32[]{:S(2)}) copy-start(bf16[128,81]{0,1:T(8,128)(2,1)} %param.10) | copy-start | bytes 62212
  15.4 29.9 %copy-start.13 = (bf16[16,1,16,32]{3,2,1,0:T(8,128)(2,1)S(1)}, bf16[16,1,16,32]{3,2,1,0:T(8,128)(2,1)}, u32[]{:S(2)}) copy-start(bf16[16,1,16,32]{3,2,1,0:T(8,128)(2,1)} %param.12) | copy-start | bytes 49156
  15.4 40.7 %collective-permute-start.1 = (bf16[1552,128]{1,0:T(8,128)(2,1)}, bf16[1552,128]{1,0:T(8,128)(2,1)S(1)}, u32[]{:S(2)}, u32[]{:S(2)}) collective-permute-start(bf16[1552,128]{1,0:T(8,128)(2,1)} %get-tuple-element.22), channel_id=1, source_target_pairs={{0,384},{128,0},{256,128},{384,256},{1,385},{129,1},{257,129},{385... | collective-permute-start | bytes 1191944 | tf_op jit(solution)/shard_map/ppermute | solution.py:218
  25.3 30.8 %collective-permute-start = (bf16[1552,128]{1,0:T(8,128)(2,1)}, bf16[1552,128]{1,0:T(8,128)(2,1)S(1)}, u32[]{:S(2)}, u32[]{:S(2)}) collective-permute-start(bf16[1552,128]{1,0:T(8,128)(2,1)} %get-tuple-element.21.c0), channel_id=1, source_target_pairs={{0,128},{128,256},{256,384},{384,0},{1,129},{129,257},{257,385},{3... | collective-permute-start | bytes 1191944 | tf_op jit(solution)/shard_map/ppermute | solution.py:218
  45.1 7.8 %copy-start.2 = (bf16[1024,192]{1,0:T(8,128)(2,1)S(1)}, bf16[1024,192]{1,0:T(8,128)(2,1)}, u32[]{:S(2)}) copy-start(bf16[1024,192]{1,0:T(8,128)(2,1)} %copy-done.1) | copy-start | bytes 1179652
  45.1 7.8 %copy-start.4 = (bf16[1024,192]{1,0:T(8,128)(2,1)S(1)}, bf16[1024,192]{1,0:T(8,128)(2,1)}, u32[]{:S(2)}) copy-start(bf16[1024,192]{1,0:T(8,128)(2,1)} %copy-done.3) | copy-start | bytes 1179652
  52.9 3.3 %copy-start.12 = (bf16[3,1,128,256]{3,2,1,0:T(8,128)(2,1)S(1)}, bf16[3,1,128,256]{3,2,1,0:T(8,128)(2,1)}, u32[]{:S(2)}) copy-start(bf16[3,1,128,256]{3,2,1,0:T(8,128)(2,1)} %param.9) | copy-start | bytes 589828
  56.2 8.5 %collective-permute-start.3 = (bf16[3,1,130,256]{3,2,1,0:T(8,128)(2,1)S(1)}, bf16[3,1,130,256]{3,2,1,0:T(8,128)(2,1)S(1)}, u32[]{:S(2)}, u32[]{:S(2)}) collective-permute-start(bf16[3,1,130,256]{3,2,1,0:T(8,128)(2,1)S(1)} %pad_maximum_fusion.v0), channel_id=1, source_target_pairs={{0,2},{1,3},{2,4},{3,5},{4,6},{5,7},{6,8},{7,9},{8,10},{9,11},{10,... | collective-permute-start | bytes 599048 | tf_op jit(solution)/shard_map/ppermute | solution.py:218
  57.5 9.9 %collective-permute-start.2 = (bf16[3,1,130,256]{3,2,1,0:T(8,128)(2,1)S(1)}, bf16[3,1,130,256]{3,2,1,0:T(8,128)(2,1)S(1)}, u32[]{:S(2)}, u32[]{:S(2)}) collective-permute-start(bf16[3,1,130,256]{3,2,1,0:T(8,128)(2,1)S(1)} %pad_maximum_fusion.v0), channel_id=1, source_target_pairs={{0,1},{1,2},{2,3},{3,4},{4,5},{5,6},{6,7},{7,8},{8,9},{9,10},{10,1... | collective-permute-start | bytes 599048 | tf_op jit(solution)/shard_map/ppermute | solution.py:218
  68.0 54.3 %all-to-all-start.1 = ((bf16[16,64,1152]{2,1,0:T(8,128)(2,1)}), bf16[16,64,1152]{2,1,0:T(8,128)(2,1)S(1)}, u32[]{:S(2)}, u32[]{:S(2)}) async-start(bf16[16,64,1152]{2,1,0:T(8,128)(2,1)} %bitcast.17), calls=%async_computation.1 | async-start | bytes 4718592 | tf_op jit(solution)/shard_map/all_to_all | solution.py:301
  82.1 22.6 %collective-permute-start.5 = (bf16[768,128]{1,0:T(8,128)(2,1)}, bf16[768,128]{1,0:T(8,128)(2,1)}, u32[]{:S(2)}, u32[]{:S(2)}) collective-permute-start(bf16[768,128]{1,0:T(8,128)(2,1)} %slice.41), channel_id=1, source_target_pairs={{0,384},{128,0},{256,128},{384,256},{1,385},{129,1},{257,129},{385... | collective-permute-start | bytes 589832 | tf_op jit(solution)/shard_map/ppermute | solution.py:218
  87.3 17.4 %collective-permute-start.4 = (bf16[768,128]{1,0:T(8,128)(2,1)}, bf16[768,128]{1,0:T(8,128)(2,1)}, u32[]{:S(2)}, u32[]{:S(2)}) collective-permute-start(bf16[768,128]{1,0:T(8,128)(2,1)} %slice.40), channel_id=1, source_target_pairs={{0,128},{128,256},{256,384},{384,0},{1,129},{129,257},{257,385},{3... | collective-permute-start | bytes 589832 | tf_op jit(solution)/shard_map/ppermute | solution.py:218
  91.4 1.0 copy-start.6
  92.3 0.9 copy-start.8
  128.6 8.5 %collective-permute-start.6 = (bf16[4,192,384]{2,1,0:T(8,128)(2,1)S(1)}, bf16[4,192,384]{2,1,0:T(8,128)(2,1)S(1)}, u32[]{:S(2)}, u32[]{:S(2)}) collective-permute-start(bf16[4,192,384]{2,1,0:T(8,128)(2,1)S(1)} %slice.49), channel_id=1, source_target_pairs={{0,1},{1,0},{2,3},{3,2},{4,5},{5,4},{6,7},{7,6},{8,9},{9,8},{10,11... | collective-permute-start | bytes 1769480 | tf_op jit(solution)/shard_map/ppermute | solution.py:218
  130.5 24.1 %all-to-all-start.2 = ((bf16[4,128,384]{2,1,0:T(8,128)(2,1)}), bf16[4,128,384]{2,1,0:T(8,128)(2,1)S(1)}, u32[]{:S(2)}, u32[]{:S(2)}) async-start(bf16[4,128,384]{2,1,0:T(8,128)(2,1)} %bitcast.18), calls=%async_computation.2 | async-start | bytes 786432 | tf_op jit(solution)/shard_map/all_to_all | solution.py:306
  137.2 12.0 %collective-permute-start.7 = (bf16[192,384]{1,0:T(8,128)(2,1)S(1)}, bf16[192,384]{1,0:T(8,128)(2,1)S(1)}, u32[]{:S(2)}, u32[]{:S(2)}) collective-permute-start(bf16[192,384]{1,0:T(8,128)(2,1)S(1)} %get-tuple-element.37), channel_id=1, source_target_pairs={{0,2},{2,4},{4,6},{6,0},{1,3},{3,5},{5,7},{7,1},{8,10},{10,12},{12... | collective-permute-start | bytes 442376 | tf_op jit(solution)/shard_map/ppermute | solution.py:218
  142.4 6.8 %collective-permute-start.9 = (bf16[192,384]{1,0:T(8,128)(2,1)S(1)}, bf16[192,384]{1,0:T(8,128)(2,1)S(1)}, u32[]{:S(2)}, u32[]{:S(2)}) collective-permute-start(bf16[192,384]{1,0:T(8,128)(2,1)S(1)} %get-tuple-element.38), channel_id=1, source_target_pairs={{0,6},{2,0},{4,2},{6,4},{1,7},{3,1},{5,3},{7,5},{8,14},{10,8},{12,... | collective-permute-start | bytes 442376 | tf_op jit(solution)/shard_map/ppermute | solution.py:218
  145.6 8.2 %collective-permute-start.8 = (bf16[192,384]{1,0:T(8,128)(2,1)S(1)}, bf16[192,384]{1,0:T(8,128)(2,1)S(1)}, u32[]{:S(2)}, u32[]{:S(2)}) collective-permute-start(bf16[192,384]{1,0:T(8,128)(2,1)S(1)} %get-tuple-element.39), channel_id=1, source_target_pairs={{0,4},{2,6},{4,0},{6,2},{1,5},{3,7},{5,1},{7,3},{8,12},{10,14},{12... | collective-permute-start | bytes 442376 | tf_op jit(solution)/shard_map/ppermute | solution.py:218
  154.6 25.8 %all-to-all-start.3 = ((bf16[16,12,384]{2,1,0:T(8,128)(2,1)}), bf16[16,12,384]{2,1,0:T(8,128)(2,1)S(1)}, u32[]{:S(2)}, u32[]{:S(2)}) async-start(bf16[16,12,384]{2,1,0:T(8,128)(2,1)} %reshape.65), calls=%async_computation.3 | async-start | bytes 393216 | tf_op jit(solution)/shard_map/all_to_all | solution.py:329
  (5 other events, 3.9 us)
